TPU v7x, 512 devices: a whole 4x8x8 slice. The times are simulated.
512 devices in a mesh: space: 64 (over z, y_hi, core), sample: 8 (over x, y_lo).
Axes of the slice: x: 4, y: 8 (y_hi: 4, y_lo: 2; y = y_hi * 2 + y_lo), z: 8, core: 2. Of those that a mesh axis runs over, the one named last changes fastest.
Arguments:
- density: float32 [64, 128, 256], P('space'), may hold values from 0.05 to 1
- fixed_mask: int32 [64, 128, 256], P('space'), may hold values 0 or 1
- load_mask: int32 [64, 128, 256], P('space'), may hold values 0 or 1
- load_fields: bfloat16 [2, 8, 64, 128, 256], P(None, None, 'space'), may hold values from -6 to 6
- angle_index: int32 [8], P('sample'), may hold values from 0 to 15
Outputs:
- displacement: float32 [8, 8, 64, 128, 256], P('sample', None, 'space')
- filtered: float32 [64, 128, 256], P('space')
All inputs are finite; a program needn't handle non-finite values. No bound on the sum of `fixed_mask` or of `load_mask` on one device may be relied on, other than what follows from the above.
Results may differ from a plain program's by a relative error of at most 0.00075.
Values sent between devices are 32-bit elements; how exact they have to be, the bound alone decides.
A program may use at most 64 MiB of HBM per device.

v0:
```python
import math

import jax
import jax.numpy as jnp
from jax import lax
from jax.sharding import PartitionSpec as P

ITERS = 2
SWEEPS = 2
ANGLES = 16


young_floor = 0.001
filter_weight = 2.25


def extended(cells, sides, width):
    for axis, dim in sides:
        count = lax.axis_size(axis)
        ends = count - 1
        head = lax.slice_in_dim(cells, 0, width, axis=dim)
        tail = lax.slice_in_dim(cells, cells.shape[dim] - width, cells.shape[dim], axis=dim)
        cells = jnp.concatenate(
            [
                lax.ppermute(tail, axis, [(i, (i + 1) % count) for i in range(ends)]),
                cells,
                lax.ppermute(head, axis, [((i + 1) % count, i) for i in range(ends)]),
            ],
            axis=dim,
        )
    return cells


def neighbours(padded):
    return [
        padded[..., 2:, 1:-1, 1:-1],
        padded[..., :-2, 1:-1, 1:-1],
        padded[..., 1:-1, 2:, 1:-1],
        padded[..., 1:-1, :-2, 1:-1],
        padded[..., 1:-1, 1:-1, 2:],
        padded[..., 1:-1, 1:-1, :-2],
    ]


def pad_yz(field):
    return jnp.pad(field, [(0, 0)] * (field.ndim - 2) + [(1, 1), (1, 1)])


def stiffness(modulus_rims):
    padded = pad_yz(modulus_rims)
    centre = padded[1:-1, 1:-1, 1:-1]
    return [2.0 * centre * other / (centre + other) for other in neighbours(padded)]


def operate(field_rims, field, springs, free_cell, fixed_cell):
    padded = pad_yz(field_rims)
    summed = jnp.zeros_like(field)
    for spring, other in zip(springs, neighbours(padded)):
        summed = summed + spring * (field - other)
    return free_cell * summed + fixed_cell * field


def inner_sum(left, right):
    return jnp.einsum("saxyz,sbxyz->sab", left, right, precision=lax.Precision.HIGHEST)


def combine(field, mixing):
    return jnp.einsum("saxyz,sab->sbxyz", field, mixing, precision=lax.Precision.HIGHEST)


def block_solve(gram_now, rhs):
    factor = jnp.linalg.cholesky(gram_now)
    lower_part = lax.linalg.triangular_solve(factor, rhs, left_side=True, lower=True)
    return lax.linalg.triangular_solve(
        factor, lower_part, left_side=True, lower=True, transpose_a=True
    )


def smooth_step(padded, source):
    beside_all = sum(neighbours(padded))
    return (source + filter_weight * beside_all) / (1.0 + 6.0 * filter_weight)


def body(density, fixed_mask, load_mask, load_fields, angle_index):
    fixed_cell = fixed_mask.astype(jnp.float32)
    free_cell = 1.0 - fixed_cell
    modulus = young_floor + (1.0 - young_floor) * density**3
    modulus_rims = extended(modulus, (("space", 0),), 1)
    springs = stiffness(modulus_rims)
    inverse_diag = 1.0 / (free_cell * sum(springs) + fixed_cell)
    angle_rad = angle_index.astype(jnp.float32) * (2.0 * math.pi / ANGLES)
    load_x = load_fields[0].astype(jnp.float32)
    load_y = load_fields[1].astype(jnp.float32)
    load_cells = load_mask.astype(jnp.float32) * free_cell
    forces = load_cells * (
        jnp.cos(angle_rad)[:, None, None, None, None] * load_x[None]
        + jnp.sin(angle_rad)[:, None, None, None, None] * load_y[None]
    )
    solution = jnp.zeros_like(forces)
    residual = forces
    precond = inverse_diag * residual
    direction = precond
    gram_now = lax.psum(inner_sum(residual, precond), "space")
    for iteration in range(ITERS):
        padded = extended(direction, (("space", 2),), 1)
        applied = operate(padded, direction, springs, free_cell, fixed_cell)
        curv_gram = lax.psum(inner_sum(direction, applied), "space")
        step_mix = block_solve(curv_gram, gram_now)
        solution = solution + combine(direction, step_mix)
        residual = residual - combine(applied, step_mix)
        if iteration + 1 < ITERS:
            precond = inverse_diag * residual
            new_gram = lax.psum(inner_sum(residual, precond), "space")
        if iteration + 1 < ITERS:
            keep_mix = block_solve(gram_now, new_gram)
            direction = precond + combine(direction, keep_mix)
            gram_now = new_gram
    solution_padded = extended(solution, (("space", 2),), 1)
    padded = pad_yz(solution_padded)
    local_energy = jnp.zeros_like(modulus)
    for spring, other in zip(springs, neighbours(padded)):
        weight = 0.5 * (spring / modulus) ** 2
        local_energy = local_energy + weight * jnp.sum((solution - other) ** 2, axis=(0, 1))
    samples_all = lax.axis_size("sample") * angle_index.shape[0]
    energy_sum = lax.psum(local_energy, "sample")
    sensitivity = -3.0 * density**2 * (1.0 - young_floor) * energy_sum / samples_all
    current = sensitivity
    for sweep_no in range(SWEEPS):
        rims = extended(current, (("space", 0),), 1)
        current = smooth_step(pad_yz(rims), sensitivity)
    return (solution, current)


def solution(mesh):
    in_specs = (
        P("space", None, None),
        P("space", None, None),
        P("space", None, None),
        P(None, None, "space", None, None),
        P("sample"),
    )
    out_specs = (P("sample", None, "space", None, None), P("space", None, None))
    return jax.shard_map(body, mesh=mesh, in_specs=in_specs, out_specs=out_specs, check_vma=False)
```

profile of v0, /device:TPU:1, one launch (start us, length us, event | category | flops | bytes accessed | tf_op | source)
XLA Modules:
  0.0 691.5 jit_solution(6053417201530899255)
XLA Ops:
  7.2 1.0 fusion.76
  8.2 8.8 %collective-permute-start = (f32[1,128,256]{2,1,0:T(8,128)S(1)}, f32[1,128,256]{2,1,0:T(8,128)S(1)}, u32[]{:S(2)}, u32[]{:S(2)}) collective-permute-start(f32[1,128,256]{2,1,0:T(8,128)S(1)} %fusion.76), channel_id=1, source_target_pairs={{8,0},{16,8},{24,16},{32,24},{40,32},{48,40},{56,48},{64,56},{72,6... | collective-permute-start | bytes 393224 | tf_op jit(solution)/shard_map/ppermute | solution.py:27
  17.0 1.9 collective-permute-start.1
  18.9 1.3 fusion.119
  21.1 0.2 select_maximum_fusion.10
  21.3 1.5 fusion.118
  22.9 0.7 multiply_multiply_fusion
  23.6 2.4 collective-permute-start.2
  26.1 4.5 collective-permute-start.3
  30.6 2.6 convolution_bitcast_fusion.4
  33.2 17.0 %collective-permute-done.2 = f32[1,8,1,128,256]{4,1,3,2,0:T(8,128)S(1)} collective-permute-done((f32[1,8,1,128,256]{4,1,3,2,0:T(8,128)S(1)}, f32[1,8,1,128,256]{4,1,3,2,0:T(8,128)S(1)}, u32[]{:S(2)}, u32[]{:S(2)}) %collective-permute-start.2) | collective-permute-done | bytes 1048608 | tf_op jit(solution)/shard_map/ppermute | solution.py:27
  50.2 2.3 select_maximum_fusion.4
  52.6 1.3 fusion.36
  53.9 2.4 convolution_bitcast_fusion.5
  56.3 146.3 %all-reduce.6 = (f32[1,8,8]{1,2,0:T(8,128)S(1)}, f32[1,8,8]{1,2,0:T(8,128)S(1)}) all-reduce(f32[1,8,8]{1,2,0:T(8,128)S(1)} %convolution_bitcast_fusion.5, f32[1,8,8]{1,2,0:T(8,128)S(1)} %convolution_bitcast_fusion.4), channel_id=1, replica_groups=mesh['space'=64,'sample'=8] {'space'}, use_global_device_ids=true, to_apply=%region_0.1 | all-reduce | flops 128 | bytes 1024 | tf_op jit(solution)/shard_map/psum | solution.py:107
  202.7 0.7 custom-call.15
  203.5 0.7 compare_reduce_fusion.2
  204.1 0.6 fusion.95
  204.7 0.6 custom-call.17
  205.4 0.2 fusion.104
  205.7 2.8 convolution_subtract_fusion
  208.5 2.4 fusion.6
  210.9 140.8 %psum.37 = f32[1,8,8]{2,1,0:T(8,128)S(1)} all-reduce(f32[1,8,8]{2,1,0:T(8,128)S(1)} %fusion.6), channel_id=1, replica_groups=mesh['space'=64,'sample'=8] {'space'}, use_global_device_ids=true, to_apply=%region_4.0 | all-reduce | flops 64 | bytes 512 | tf_op jit(solution)/shard_map/psum | solution.py:113
  351.6 0.7 custom-call.18
  352.4 0.6 compare_reduce_fusion.1
  353.0 0.6 fusion.96
  353.7 0.6 custom-call.20
  354.3 0.2 fusion.101
  354.7 1.1 multiply_add_fusion
  355.8 2.7 collective-permute-start.4
  358.5 3.9 collective-permute-start.5
  362.4 1.0 fusion.46
  363.5 13.9 %collective-permute-done.4 = f32[1,8,1,128,256]{4,1,3,2,0:T(8,128)S(1)} collective-permute-done((f32[1,8,1,128,256]{4,1,3,2,0:T(8,128)S(1)}, f32[1,8,1,128,256]{4,1,3,2,0:T(8,128)S(1)}, u32[]{:S(2)}, u32[]{:S(2)}) %collective-permute-start.4) | collective-permute-done | bytes 1048608 | tf_op jit(solution)/shard_map/ppermute | solution.py:27
  377.4 7.9 %collective-permute-done.5 = f32[1,8,1,128,256]{4,1,3,2,0:T(8,128)S(1)} collective-permute-done((f32[1,8,1,128,256]{4,1,3,2,0:T(8,128)S(1)}, f32[1,8,1,128,256]{4,1,3,2,0:T(8,128)S(1)}, u32[]{:S(2)}, u32[]{:S(2)}) %collective-permute-start.5) | collective-permute-done | bytes 1048608 | tf_op jit(solution)/shard_map/ppermute | solution.py:25
  385.3 2.3 select_maximum_fusion.2
  387.7 2.9 convolution_bitcast_fusion.1
  390.5 135.2 %psum.38 = f32[1,8,8]{1,2,0:T(8,128)S(1)} all-reduce(f32[1,8,8]{1,2,0:T(8,128)S(1)} %convolution_bitcast_fusion.1), channel_id=1, replica_groups=mesh['space'=64,'sample'=8] {'space'}, use_global_device_ids=true, to_apply=%region_5.0 | all-reduce | flops 64 | bytes 512 | tf_op jit(solution)/shard_map/psum | solution.py:107
  525.8 0.7 custom-call.21
  526.5 0.6 compare_reduce_fusion
  527.2 0.6 fusion.97
  527.8 0.6 custom-call.23
  528.5 0.2 fusion.98
  528.8 1.1 fusion.5
  529.9 5.7 collective-permute-start.6
  535.6 1.9 collective-permute-start.7
  537.5 13.9 %collective-permute-done.6 = f32[1,8,1,128,256]{4,1,3,2,0:T(8,128)S(1)} collective-permute-done((f32[1,8,1,128,256]{4,1,3,2,0:T(8,128)S(1)}, f32[1,8,1,128,256]{4,1,3,2,0:T(8,128)S(1)}, u32[]{:S(2)}, u32[]{:S(2)}) %collective-permute-start.6) | collective-permute-done | bytes 1048608 | tf_op jit(solution)/shard_map/ppermute | solution.py:27
  551.4 8.3 %collective-permute-done.7 = f32[1,8,1,128,256]{4,1,3,2,0:T(8,128)S(1)} collective-permute-done((f32[1,8,1,128,256]{4,1,3,2,0:T(8,128)S(1)}, f32[1,8,1,128,256]{4,1,3,2,0:T(8,128)S(1)}, u32[]{:S(2)}, u32[]{:S(2)}) %collective-permute-start.7) | collective-permute-done | bytes 1048608 | tf_op jit(solution)/shard_map/ppermute | solution.py:25
  559.7 2.3 select_maximum_fusion
  562.1 2.0 fusion.16
  564.1 1.0 fusion.85
  565.1 91.9 %all-reduce.9.cloned.1.call-done = f32[1,128,256]{2,1,0:T(8,128)} async-done(((f32[1,128,256]{2,1,0:T(8,128)}), f32[1,128,256]{2,1,0:T(8,128)}) %all-reduce.9.cloned.1.call-update) | async-done | bytes 131088 | tf_op jit(solution)/shard_map/psum | solution.py:125
  657.0 0.9 fusion.78
  657.9 7.5 %collective-permute-start.8 = (f32[1,128,256]{2,1,0:T(8,128)S(1)}, f32[1,128,256]{2,1,0:T(8,128)S(1)}, u32[]{:S(2)}, u32[]{:S(2)}) collective-permute-start(f32[1,128,256]{2,1,0:T(8,128)S(1)} %fusion.78), channel_id=1, source_target_pairs={{8,0},{16,8},{24,16},{32,24},{40,32},{48,40},{56,48},{64,56},{72,6... | collective-permute-start | bytes 393224 | tf_op jit(solution)/shard_map/ppermute | solution.py:27
  665.5 3.9 collective-permute-start.9
  669.4 0.7 collective-permute-done.8
  670.1 2.5 collective-permute-done.9
  672.6 0.2 select_maximum_fusion.8
  672.8 0.2 fusion.84
  673.0 1.9 collective-permute-start.10
  675.0 5.3 collective-permute-start.11
  680.3 1.3 copy.26
  681.6 2.0 collective-permute-done.11
  683.6 0.2 select_maximum_fusion.6
  683.8 0.8 fusion.81
  (64 shorter events, 1.0 us)
Async XLA Ops:
  7.2 23.4 %copy-start.22 = (s32[1,128,256]{2,1,0:T(8,128)S(1)}, s32[1,128,256]{2,1,0:T(8,128)}, u32[]{:S(2)}) copy-start(s32[1,128,256]{2,1,0:T(8,128)} %param.11) | copy-start | bytes 393220
  7.2 649.8 %all-reduce.9.cloned.1.call-start = ((), (), s32[]{:S(2)}) async-start(), calls=%async_computation | async-start | bytes 262144 | tf_op jit(solution)/shard_map/psum | solution.py:125
  8.2 12.9 %collective-permute-start = (f32[1,128,256]{2,1,0:T(8,128)S(1)}, f32[1,128,256]{2,1,0:T(8,128)S(1)}, u32[]{:S(2)}, u32[]{:S(2)}) collective-permute-start(f32[1,128,256]{2,1,0:T(8,128)S(1)} %fusion.76), channel_id=1, source_target_pairs={{8,0},{16,8},{24,16},{32,24},{40,32},{48,40},{56,48},{64,56},{72,6... | collective-permute-start | bytes 393224 | tf_op jit(solution)/shard_map/ppermute | solution.py:27
  17.0 4.1 collective-permute-start.1
  20.2 30.0 %copy-start = (bf16[1,8,1,128,256]{4,3,2,1,0:T(8,128)(2,1)}, bf16[1,8,1,128,256]{4,3,2,1,0:T(8,128)(2,1)S(1)}, u32[]{:S(2)}) copy-start(bf16[1,8,1,128,256]{4,3,2,1,0:T(8,128)(2,1)S(1)} %get-tuple-element.15) | copy-start | bytes 1572868
  20.2 30.0 %copy-start.1 = (bf16[1,8,1,128,256]{4,3,2,1,0:T(8,128)(2,1)}, bf16[1,8,1,128,256]{4,3,2,1,0:T(8,128)(2,1)S(1)}, u32[]{:S(2)}) copy-start(bf16[1,8,1,128,256]{4,3,2,1,0:T(8,128)(2,1)S(1)} %get-tuple-element.16) | copy-start | bytes 1572868
  21.3 1.6 copy-start.2
  22.8 27.4 %copy-start.5 = (f32[128,256]{1,0:T(8,128)}, f32[128,256]{1,0:T(8,128)S(1)}, u32[]{:S(2)}) copy-start(f32[128,256]{1,0:T(8,128)S(1)} %get-tuple-element.25) | copy-start | bytes 393220
  22.9 29.7 %copy-start.6 = (f32[128,256]{1,0:T(8,128)}, f32[128,256]{1,0:T(8,128)S(1)}, u32[]{:S(2)}) copy-start(f32[128,256]{1,0:T(8,128)S(1)} %get-tuple-element.17) | copy-start | bytes 393220
  22.9 29.7 %copy-start.8 = (f32[128,256]{1,0:T(8,128)}, f32[128,256]{1,0:T(8,128)S(1)}, u32[]{:S(2)}) copy-start(f32[128,256]{1,0:T(8,128)S(1)} %get-tuple-element.18) | copy-start | bytes 393220
  22.9 29.7 %copy-start.10 = (f32[128,256]{1,0:T(8,128)}, f32[128,256]{1,0:T(8,128)S(1)}, u32[]{:S(2)}) copy-start(f32[128,256]{1,0:T(8,128)S(1)} %get-tuple-element.20) | copy-start | bytes 393220
  22.9 29.7 %copy-start.12 = (f32[128,256]{1,0:T(8,128)}, f32[128,256]{1,0:T(8,128)S(1)}, u32[]{:S(2)}) copy-start(f32[128,256]{1,0:T(8,128)S(1)} %get-tuple-element.21) | copy-start | bytes 393220
  22.9 29.7 %copy-start.14 = (f32[128,256]{1,0:T(8,128)}, f32[128,256]{1,0:T(8,128)S(1)}, u32[]{:S(2)}) copy-start(f32[128,256]{1,0:T(8,128)S(1)} %get-tuple-element.22) | copy-start | bytes 393220
  22.9 29.7 %copy-start.16 = (f32[128,256]{1,0:T(8,128)}, f32[128,256]{1,0:T(8,128)S(1)}, u32[]{:S(2)}) copy-start(f32[128,256]{1,0:T(8,128)S(1)} %get-tuple-element.23) | copy-start | bytes 393220
  22.9 29.7 %copy-start.18 = (f32[128,256]{1,0:T(8,128)}, f32[128,256]{1,0:T(8,128)S(1)}, u32[]{:S(2)}) copy-start(f32[128,256]{1,0:T(8,128)S(1)} %get-tuple-element.24) | copy-start | bytes 393220
  23.6 26.6 %collective-permute-start.2 = (f32[1,8,1,128,256]{4,1,3,2,0:T(8,128)S(1)}, f32[1,8,1,128,256]{4,1,3,2,0:T(8,128)S(1)}, u32[]{:S(2)}, u32[]{:S(2)}) collective-permute-start(f32[1,8,1,128,256]{4,1,3,2,0:T(8,128)S(1)} %multiply_multiply_fusion), channel_id=1, source_target_pairs={{8,0},{16,8},{24,16},{32,24},{40,32},{48,40},{56,48},{64,56},{72,6... | collective-permute-start | bytes 3145736 | tf_op jit(solution)/shard_map/ppermute | solution.py:27
  26.1 24.2 %collective-permute-start.3 = (f32[1,8,1,128,256]{4,1,3,2,0:T(8,128)S(1)}, f32[1,8,1,128,256]{4,1,3,2,0:T(8,128)S(1)}, u32[]{:S(2)}, u32[]{:S(2)}) collective-permute-start(f32[1,8,1,128,256]{4,1,3,2,0:T(8,128)S(1)} %multiply_multiply_fusion), channel_id=1, source_target_pairs={{0,8},{8,16},{16,24},{24,32},{32,40},{40,48},{48,56},{56,64},{64,7... | collective-permute-start | bytes 3145736 | tf_op jit(solution)/shard_map/ppermute | solution.py:25
  30.6 22.0 %copy-start.20 = (f32[128,256]{1,0:T(8,128)}, f32[128,256]{1,0:T(8,128)S(1)}, u32[]{:S(2)}) copy-start(f32[128,256]{1,0:T(8,128)S(1)} %convert_bitcast_fusion) | copy-start | bytes 393220
  355.8 31.9 %copy-start.7 = (f32[128,256]{1,0:T(8,128)S(1)}, f32[128,256]{1,0:T(8,128)}, u32[]{:S(2)}) copy-start(f32[128,256]{1,0:T(8,128)} %copy-done.6) | copy-start | bytes 393220
  355.8 31.9 %copy-start.9 = (f32[128,256]{1,0:T(8,128)S(1)}, f32[128,256]{1,0:T(8,128)}, u32[]{:S(2)}) copy-start(f32[128,256]{1,0:T(8,128)} %copy-done.8) | copy-start | bytes 393220
  355.8 31.9 %copy-start.11 = (f32[128,256]{1,0:T(8,128)S(1)}, f32[128,256]{1,0:T(8,128)}, u32[]{:S(2)}) copy-start(f32[128,256]{1,0:T(8,128)} %copy-done.10) | copy-start | bytes 393220
  355.8 31.9 %copy-start.13 = (f32[128,256]{1,0:T(8,128)S(1)}, f32[128,256]{1,0:T(8,128)}, u32[]{:S(2)}) copy-start(f32[128,256]{1,0:T(8,128)} %copy-done.12) | copy-start | bytes 393220
  355.8 31.9 %copy-start.15 = (f32[128,256]{1,0:T(8,128)S(1)}, f32[128,256]{1,0:T(8,128)}, u32[]{:S(2)}) copy-start(f32[128,256]{1,0:T(8,128)} %copy-done.14) | copy-start | bytes 393220
  355.8 31.9 %copy-start.17 = (f32[128,256]{1,0:T(8,128)S(1)}, f32[128,256]{1,0:T(8,128)}, u32[]{:S(2)}) copy-start(f32[128,256]{1,0:T(8,128)} %copy-done.16) | copy-start | bytes 393220
  355.8 31.9 %copy-start.19 = (f32[128,256]{1,0:T(8,128)S(1)}, f32[128,256]{1,0:T(8,128)}, u32[]{:S(2)}) copy-start(f32[128,256]{1,0:T(8,128)} %copy-done.18) | copy-start | bytes 393220
  355.8 31.9 %copy-start.21 = (f32[128,256]{1,0:T(8,128)S(1)}, f32[128,256]{1,0:T(8,128)}, u32[]{:S(2)}) copy-start(f32[128,256]{1,0:T(8,128)} %copy-done.20) | copy-start | bytes 393220
  355.8 21.6 %collective-permute-start.4 = (f32[1,8,1,128,256]{4,1,3,2,0:T(8,128)S(1)}, f32[1,8,1,128,256]{4,1,3,2,0:T(8,128)S(1)}, u32[]{:S(2)}, u32[]{:S(2)}) collective-permute-start(f32[1,8,1,128,256]{4,1,3,2,0:T(8,128)S(1)} %bitcast.182), channel_id=1, source_target_pairs={{8,0},{16,8},{24,16},{32,24},{40,32},{48,40},{56,48},{64,56},{72,6... | collective-permute-start | bytes 3145736 | tf_op jit(solution)/shard_map/ppermute | solution.py:27
  358.5 26.8 %collective-permute-start.5 = (f32[1,8,1,128,256]{4,1,3,2,0:T(8,128)S(1)}, f32[1,8,1,128,256]{4,1,3,2,0:T(8,128)S(1)}, u32[]{:S(2)}, u32[]{:S(2)}) collective-permute-start(f32[1,8,1,128,256]{4,1,3,2,0:T(8,128)S(1)} %bitcast.183), channel_id=1, source_target_pairs={{0,8},{8,16},{16,24},{24,32},{32,40},{40,48},{48,56},{56,64},{64,7... | collective-permute-start | bytes 3145736 | tf_op jit(solution)/shard_map/ppermute | solution.py:25
  529.9 21.5 %collective-permute-start.6 = (f32[1,8,1,128,256]{4,1,3,2,0:T(8,128)S(1)}, f32[1,8,1,128,256]{4,1,3,2,0:T(8,128)S(1)}, u32[]{:S(2)}, u32[]{:S(2)}) collective-permute-start(f32[1,8,1,128,256]{4,1,3,2,0:T(8,128)S(1)} %fusion.5), channel_id=1, source_target_pairs={{8,0},{16,8},{24,16},{32,24},{40,32},{48,40},{56,48},{64,56},{72,6... | collective-permute-start | bytes 3145736 | tf_op jit(solution)/shard_map/ppermute | solution.py:27
  535.6 24.2 %collective-permute-start.7 = (f32[1,8,1,128,256]{4,1,3,2,0:T(8,128)S(1)}, f32[1,8,1,128,256]{4,1,3,2,0:T(8,128)S(1)}, u32[]{:S(2)}, u32[]{:S(2)}) collective-permute-start(f32[1,8,1,128,256]{4,1,3,2,0:T(8,128)S(1)} %fusion.5), channel_id=1, source_target_pairs={{0,8},{8,16},{16,24},{24,32},{32,40},{40,48},{48,56},{56,64},{64,7... | collective-permute-start | bytes 3145736 | tf_op jit(solution)/shard_map/ppermute | solution.py:25
  562.1 2.0 copy-start.3
  562.1 2.0 copy-start.4
  657.9 12.2 %collective-permute-start.8 = (f32[1,128,256]{2,1,0:T(8,128)S(1)}, f32[1,128,256]{2,1,0:T(8,128)S(1)}, u32[]{:S(2)}, u32[]{:S(2)}) collective-permute-start(f32[1,128,256]{2,1,0:T(8,128)S(1)} %fusion.78), channel_id=1, source_target_pairs={{8,0},{16,8},{24,16},{32,24},{40,32},{48,40},{56,48},{64,56},{72,6... | collective-permute-start | bytes 393224 | tf_op jit(solution)/shard_map/ppermute | solution.py:27
  665.5 7.2 %collective-permute-start.9 = (f32[1,128,256]{2,1,0:T(8,128)S(1)}, f32[1,128,256]{2,1,0:T(8,128)S(1)}, u32[]{:S(2)}, u32[]{:S(2)}) collective-permute-start(f32[1,128,256]{2,1,0:T(8,128)S(1)} %fusion.78), channel_id=1, source_target_pairs={{0,8},{8,16},{16,24},{24,32},{32,40},{40,48},{48,56},{56,64},{64,7... | collective-permute-start | bytes 393224 | tf_op jit(solution)/shard_map/ppermute | solution.py:25
  673.0 8.5 %collective-permute-start.10 = (f32[1,128,256]{2,1,0:T(8,128)S(1)}, f32[1,128,256]{2,1,0:T(8,128)S(1)}, u32[]{:S(2)}, u32[]{:S(2)}) collective-permute-start(f32[1,128,256]{2,1,0:T(8,128)S(1)} %fusion.84), channel_id=1, source_target_pairs={{8,0},{16,8},{24,16},{32,24},{40,32},{48,40},{56,48},{64,56},{72,6... | collective-permute-start | bytes 393224 | tf_op jit(solution)/shard_map/ppermute | solution.py:27
  675.0 8.6 %collective-permute-start.11 = (f32[1,128,256]{2,1,0:T(8,128)S(1)}, f32[1,128,256]{2,1,0:T(8,128)S(1)}, u32[]{:S(2)}, u32[]{:S(2)}) collective-permute-start(f32[1,128,256]{2,1,0:T(8,128)S(1)} %fusion.84), channel_id=1, source_target_pairs={{0,8},{8,16},{16,24},{24,32},{32,40},{40,48},{48,56},{56,64},{64,7... | collective-permute-start | bytes 393224 | tf_op jit(solution)/shard_map/ppermute | solution.py:25
Sparse Core Ops, SparseCore 0:
  565.2 91.7 all-reduce.8
where the time goes:
time: 693 us; the launch traced here: 691 us
  blocking collectives  422 us (61%)
  waiting for transfers between devices  158 us (23%)
  starting transfers between devices  50.6 us (7%)
  other arithmetic  25 us (4%)
  matrix products  17.1 us (2%)
  between operations  15.5 us (2%)
    psum x2, blocking collectives, body(): curv_gram = lax.psum(inner_sum(direction, applied), 'space')  281 us
    psum x1, blocking collectives, body(): new_gram = lax.psum(inner_sum(residual, precond), 'space')  141 us
    psum x1, waiting for transfers between devices, body(): energy_sum = lax.psum(local_energy, 'sample')  91.9 us
    ppermute x6, waiting for transfers between devices, extended(): lax.ppermute(head, axis, [((i + 1) % count, i) for i in range(ends)])  45.6 us
    ppermute x6, starting transfers between devices, extended(): lax.ppermute(head, axis, [((i + 1) % count, i) for i in range(ends)])  29 us
    ppermute x6, starting transfers between devices, extended(): lax.ppermute(tail, axis, [(i, (i + 1) % count) for i in range(ends)])  21.5 us
    ppermute x6, waiting for transfers between devices, extended(): lax.ppermute(tail, axis, [(i, (i + 1) % count) for i in range(ends)])  20.7 us
  transfers between devices with their start and end apart: 13, of which 9 were waited for; matrix products, arithmetic and copies ran while one was open for 1% of the time, Pallas kernels for 0%

commit v1 on v0

v1 whole, which is shorter than its diff:
```python
import math

import jax
import jax.numpy as jnp
from jax import lax
from jax.experimental import pallas as pl
from jax.experimental.pallas import tpu as pltpu
from jax.sharding import PartitionSpec as P

ANGLES = 16
MESH = pl.DeviceIdType.MESH
f32 = jnp.float32
bf16 = jnp.bfloat16

young_floor = 0.001
filter_weight = 2.25

NY, NZ = 128, 256
SLAB = 16
FIELDS = 16
LOADS = 8
GROUP = 8
PLANES = 64

K_TRIG = 0
K_MOD = 7
K_F = 11
K_V = 13
K_GRAM = 15
K_X = 36
K_S = 43
K_OUT = 53
COPIES = 60

SPREAD = [(d, e) for d in (-1, 0, 1) for e in (-1, 0, 1) if (d, e) != (0, 0)] + [
    (-2, 0),
    (2, 0),
]


def harmonic(a, b):
    return 2.0 * a * b / jnp.maximum(a + b, 1e-30)


def next_row(a):
    return pltpu.roll(a, a.shape[0] - 1, 0)


def last_row(a):
    return pltpu.roll(a, 1, 0)


def next_col(a):
    return pltpu.roll(a, a.shape[1] - 1, 1)


def last_col(a):
    return pltpu.roll(a, 1, 1)


def split(a):
    high = a.astype(bf16)
    return high, (a - high.astype(f32)).astype(bf16)


def spread_row(a, k):
    return jnp.broadcast_to(a[k : k + 1, :], a.shape)


def spread_col(a, k):
    return jnp.broadcast_to(a[:, k : k + 1], a.shape)


def product(a, b):
    out = []
    for i in range(LOADS):
        row = spread_row(a[i], 0) * b[0]
        for k in range(1, LOADS):
            row = row + spread_row(a[i], k) * b[k]
        out.append(row)
    return out


def product_t(a, b):
    out = []
    for i in range(LOADS):
        row = spread_row(a[0], i) * b[0]
        for k in range(1, LOADS):
            row = row + spread_row(a[k], i) * b[k]
        out.append(row)
    return out


def plus(a, b):
    return [x + y for x, y in zip(a, b)]


def minus(a, b):
    return [x - y for x, y in zip(a, b)]


def solve(a, b):
    a, b = list(a), list(b)
    for k in range(LOADS):
        scale = 1.0 / spread_row(a[k], k)
        a[k] = a[k] * scale
        b[k] = b[k] * scale
        for i in range(LOADS):
            if i != k:
                factor = spread_row(a[i], k)
                a[i] = a[i] - factor * a[k]
                b[i] = b[i] - factor * b[k]
    return b


def kernel(
    trig_in,
    den_ref,
    fix_ref,
    mask_ref,
    load_ref,
    x_out,
    f_out,
    trig,
    mod,
    dense,
    f_own,
    f_rim,
    z_own,
    z_rim,
    coef,
    e_own,
    v_own,
    v_rim,
    gram,
    gram_in,
    x_own,
    x_send,
    q_ref,
    s_own,
    s_in,
    send_sem,
    recv_sem,
    local_sem,
):
    plane = lax.axis_index("space")
    slab = lax.axis_index("sample")
    zpos = plane // GROUP
    ypos = plane % GROUP

    def at(planes, slabs):
        return ((plane + PLANES + planes) % PLANES, (slab + GROUP + slabs) % GROUP)

    def y_mate(off):
        return (zpos * GROUP + (ypos + off) % GROUP, slab)

    def z_mate(off):
        return (((zpos + off) % GROUP) * GROUP + ypos, slab)

    def copy(src, dst, k, device):
        return pltpu.make_async_remote_copy(
            src_ref=src,
            dst_ref=dst,
            send_sem=send_sem.at[k],
            recv_sem=recv_sem.at[k],
            device_id=device,
            device_id_type=MESH,
        )

    mates = [at(0, off) for off in range(1, GROUP)]
    mates += [at(d, 0) for d in (-2, -1, 1, 2)]
    mates += [at(d, e) for d in (-1, 1) for e in (-1, 1)]
    mates += [y_mate(off) for off in range(1, GROUP)]
    mates += [z_mate(off) for off in range(1, GROUP)]
    barrier = pltpu.get_barrier_semaphore()
    for mate in mates:
        pl.semaphore_signal(barrier, inc=1, device_id=mate, device_id_type=MESH)

    before = pl.multiple_of(((slab + GROUP - 1) % GROUP) * SLAB, SLAB)
    here = pl.multiple_of(slab * SLAB, SLAB)
    after = pl.multiple_of(((slab + 1) % GROUP) * SLAB, SLAB)

    def window(ref):
        return jnp.concatenate(
            [
                ref[pl.ds(before, SLAB), :][8:],
                ref[pl.ds(here, SLAB), :],
                ref[pl.ds(after, SLAB), :][:8],
            ],
            axis=0,
        )

    row = lax.broadcasted_iota(jnp.int32, (32, NZ), 0) + (slab * SLAB - 8)
    inside = jnp.where((row >= 0) & (row < NY), 1.0, 0.0).astype(f32)
    lane = lax.broadcasted_iota(jnp.int32, (32, NZ), 1)
    not_last = jnp.where(lane < NZ - 1, 1.0, 0.0).astype(f32)
    density = window(den_ref)
    free = inside * (1.0 - window(fix_ref).astype(f32))
    loaded = free * window(mask_ref).astype(f32)
    modulus = inside * (young_floor + (1.0 - young_floor) * density * density * density)
    mod[2] = modulus
    trig[0] = trig_in[...]

    for k in range(FIELDS):
        rows = jnp.concatenate(
            [
                load_ref[k, pl.ds(before, SLAB), :].astype(f32)[12:],
                load_ref[k, pl.ds(here, SLAB), :].astype(f32),
                load_ref[k, pl.ds(after, SLAB), :].astype(f32)[:4],
            ],
            axis=0,
        )
        rows = rows * loaded[4:28]
        dense[0, 24 * k : 24 * k + 24, :] = rows[:, :128]
        dense[1, 24 * k : 24 * k + 24, :] = rows[:, 128:]
    for r in range(20):
        for h in range(2):
            f_own[r, :, 128 * h : 128 * h + 128] = dense[
                h, pl.ds(r + 2, FIELDS, stride=24), :
            ]

    pl.semaphore_wait(barrier, len(mates))

    sent = []

    def send(src, dst, k, device):
        out = copy(src, dst, k, device)
        out.start()
        sent.append(out)
        return out

    mods = [
        send(mod.at[2], mod.at[2 - d], K_MOD + n, at(d, 0))
        for n, d in enumerate((-2, -1, 1, 2))
    ]
    fs = [
        send(f_own.at[pl.ds(1, 18)], f_rim.at[0], K_F, at(-1, 0)),
        send(f_own.at[pl.ds(1, 18)], f_rim.at[1], K_F + 1, at(1, 0)),
    ]
    trigs = [
        send(trig.at[0], trig.at[off], K_TRIG + off - 1, at(0, off))
        for off in range(1, GROUP)
    ]
    for c in mods:
        c.wait_recv()

    def plane_inside(d):
        there = plane + d
        return jnp.where((there >= 0) & (there < PLANES), 1.0, 0.0).astype(f32)

    m0 = modulus
    m_up = mod[3] * plane_inside(1)
    m_up2 = mod[4] * plane_inside(2)
    m_dn = mod[1] * plane_inside(-1)
    m_dn2 = mod[0] * plane_inside(-2)
    up = harmonic(m0, m_up)
    down = harmonic(m0, m_dn)

    def flat_springs(m):
        to_next = harmonic(m, next_row(m))
        right = harmonic(m, next_col(m)) * not_last
        return to_next, last_row(to_next), right, last_col(right)

    own4 = flat_springs(m0)
    springs = (up, down) + own4
    total = up + down + own4[0] + own4[1] + own4[2] + own4[3]
    inverse = 1.0 / (free * total + (1.0 - free))

    def rim_inverse(m, beyond, between):
        a, b, c, d = flat_springs(m)
        whole = beyond + between + a + b + c + d
        return 1.0 / jnp.where(whole > 0.0, whole, 1.0)

    for n in range(6):
        coef[n] = free * springs[n]
        coef[9 + n] = springs[n]
    coef[6] = inverse
    coef[7] = rim_inverse(m_up, harmonic(m_up, m_up2), up)
    coef[8] = rim_inverse(m_dn, harmonic(m_dn, m_dn2), down)

    def along(n, w):
        return coef[n, pl.ds(w, 1), :]

    @pl.loop(0, 20)
    def _(r):
        z_own[r] = f_own[r] * along(6, r + 6)

    for c in fs:
        c.wait_recv()

    @pl.loop(0, 18)
    def _(r):
        z_rim[0, r] = f_rim[0, r] * along(7, r + 7)
        z_rim[1, r] = f_rim[1, r] * along(8, r + 7)

    @pl.loop(0, 18)
    def _(r):
        w = r + 7
        z = z_own[r + 1]
        image = (
            along(0, w) * z_rim[0, r]
            + along(1, w) * z_rim[1, r]
            + along(2, w) * z_own[r + 2]
            + along(3, w) * z_own[r]
            + along(4, w) * next_col(z)
            + along(5, w) * last_col(z)
        )
        e_own[r] = image
        v_own[r] = image * along(6, w)

    vs = [
        send(v_own.at[pl.ds(1, 16)], v_rim.at[0], K_V, at(-1, 0)),
        send(v_own.at[pl.ds(1, 16)], v_rim.at[1], K_V + 1, at(1, 0)),
    ]

    contract = (((1,), (1,)), ((), ()))

    def first_gram(c, acc):
        zh, zl = split(z_own[c + 2])
        vh, vl = split(v_own[c + 1])
        fh, fl = split(f_own[c + 2])
        eh, el = split(e_own[c + 1])
        left = jnp.concatenate([zh, vh, zl, vl], axis=0)
        right = jnp.concatenate([fh, eh, fl, el, fh, eh, fl, el], axis=0)
        return acc + lax.dot_general(left, right, contract, preferred_element_type=f32)

    acc = lax.fori_loop(0, SLAB, first_gram, jnp.zeros((64, 128), f32))
    acc = acc[:32] + acc[32:]
    acc = acc + pltpu.roll(acc, 128 - 32, 1)

    for c in vs:
        c.wait_recv()

    def second_gram(c, acc):
        w = c + 8
        v = v_own[c + 1]
        image = (
            along(0, w) * v_rim[0, c]
            + along(1, w) * v_rim[1, c]
            + along(2, w) * v_own[c + 2]
            + along(3, w) * v_own[c]
            + along(4, w) * next_col(v)
            + along(5, w) * last_col(v)
        )
        vh, vl = split(v)
        nh, nl = split(image)
        left = jnp.concatenate([vh, vl], axis=0)
        right = jnp.concatenate([nh, nl, nh, nl, nh, nl, nh, nl], axis=0)
        return acc + lax.dot_general(left, right, contract, preferred_element_type=f32)

    acc2 = lax.fori_loop(0, SLAB, second_gram, jnp.zeros((32, 128), f32))
    acc2 = acc2[:16] + acc2[16:]
    acc2 = acc2 + pltpu.roll(acc2, 128 - 16, 1)

    wide = lax.broadcasted_iota(jnp.int32, (16, 128), 1)
    packed = jnp.where(
        wide < 32,
        acc[:16],
        jnp.where(
            wide < 48,
            pltpu.roll(acc[16:], 16, 1),
            jnp.where(wide < 64, pltpu.roll(acc2, 48, 1), 0.0),
        ),
    )
    for stage, mate in enumerate((lambda off: at(0, off), y_mate, z_mate)):
        gram[stage] = packed
        arriving = [
            send(
                gram.at[stage],
                gram_in.at[stage, off - 1],
                K_GRAM + 7 * stage + off - 1,
                mate(off),
            )
            for off in range(1, GROUP)
        ]
        for n, c in enumerate(arriving):
            c.wait_recv()
            packed = packed + gram_in[stage, n]

    narrow = lax.broadcasted_iota(jnp.int32, (8, 128), 1)
    for c in trigs:
        c.wait_recv()
    cosine = jnp.zeros((8, 128), f32)
    sine = jnp.zeros((8, 128), f32)
    for off in range(GROUP):
        mine = narrow % GROUP == (slab + GROUP - off) % GROUP
        cosine = jnp.where(mine, trig[off, :8, :], cosine)
        sine = jnp.where(mine, trig[off, 8:, :], sine)
    cc, cs, ss = cosine * cosine, cosine * sine, sine * sine

    mixed = packed[8:] + pltpu.roll(packed[:8], 128 - 8, 1)

    def matrix(first):
        rows = []
        for a in range(LOADS):
            rows.append(
                cc * spread_col(packed[:8], first + a)
                + cs * spread_col(mixed, first + a)
                + ss * spread_col(packed[8:], first + 8 + a)
            )
        return rows

    g0, sm, ym, tm = matrix(0), matrix(16), matrix(32), matrix(48)
    cm = minus(g0, sm)
    e = solve(cm, sm)
    level = lax.broadcasted_iota(jnp.int32, (8, 128), 0)
    p = [e[i] + jnp.where(level == i, 1.0, 0.0).astype(f32) for i in range(LOADS)]
    g1 = minus(
        product_t(p, minus(product(ym, p), product(sm, e))),
        product_t(e, minus(product(sm, p), product(g0, e))),
    )
    q = minus(solve(g0, g1), e)
    smy = minus(sm, ym)
    curv = plus(
        product_t(q, plus(product(cm, q), product(smy, p))),
        product_t(p, plus(product(smy, q), product(minus(ym, tm), p))),
    )
    alpha = solve(curv, g1)
    on_z = plus(p, product(q, alpha))
    on_v = product(p, alpha)

    place = narrow % 32
    tiles = []
    for s in range(GROUP):
        tile = jnp.zeros((8, 128), f32)
        for a in range(LOADS):
            tile = jnp.where(
                (place < 16) & (place % 8 == a), spread_col(on_z[a], s), tile
            )
            tile = jnp.where(
                (place >= 16) & (place % 8 == a), spread_col(on_v[a], s), tile
            )
        turn = jnp.where(
            place % 16 < 8, spread_col(cosine, s), spread_col(sine, s)
        )
        tiles.append(tile * turn)
    mix = jnp.concatenate(tiles, axis=0)
    mix_high, mix_low = split(mix)
    lane64 = lax.broadcasted_iota(jnp.int32, (64, 128), 1)
    mix = jnp.where(lane64 < 64, mix_high.astype(f32), mix_low.astype(f32)).astype(bf16)

    def iterates(z, v):
        zh, zl = split(z)
        vh, vl = split(v)
        basis = jnp.concatenate([zh, vh, zl, vl, zh, vh, zl, vl], axis=0)
        return jnp.dot(mix, basis, preferred_element_type=f32)

    @pl.loop(0, 18)
    def _(r):
        x = iterates(z_own[r + 1], v_own[r])
        for h in range(2):
            x_own[h, pl.ds(pl.multiple_of(r * 64, 64), 64), :] = x[
                :, 128 * h : 128 * h + 128
            ]

    for s in range(GROUP):
        for b in range(LOADS):
            for h in range(2):
                x_send[s, b, :, 128 * h : 128 * h + 128] = x_own[
                    h, pl.ds(64 + 8 * s + b, SLAB, stride=64), :
                ]

    rows_here = pl.ds(here, SLAB)
    keep = pltpu.make_async_copy(x_send.at[slab], x_out.at[:, rows_here, :], local_sem)
    keep.start()
    xs = [
        send(
            x_send.at[(slab + off) % GROUP],
            x_out.at[:, rows_here, :],
            K_X + off - 1,
            at(0, off),
        )
        for off in range(1, GROUP)
    ]

    def squares(a, b):
        d = a - b
        return jnp.sum(d * d, axis=0, keepdims=True)

    def x_row(r):
        rows = pl.ds(pl.multiple_of(r * 64, 64), 64)
        return jnp.concatenate([x_own[0, rows, :], x_own[1, rows, :]], axis=1)

    @pl.loop(0, 17)
    def _(r):
        q_ref[2, pl.ds(r, 1), :] = squares(x_row(r), x_row(r + 1))

    @pl.loop(0, 16)
    def _(c):
        x = x_row(c + 1)
        q_ref[0, pl.ds(c, 1), :] = squares(x, iterates(z_rim[0, c + 1], v_rim[0, c]))
        q_ref[1, pl.ds(c, 1), :] = squares(x, iterates(z_rim[1, c + 1], v_rim[1, c]))
        q_ref[3, pl.ds(c, 1), :] = squares(x, next_col(x))

    core = slice(8, 24)
    softness = 1.0 / m0[core]

    def weight(n):
        ratio = coef[9 + n][core] * softness
        return 0.5 * ratio * ratio

    q_y = q_ref[2]
    q_z = q_ref[3][:16]
    energy = (
        weight(0) * q_ref[0][:16]
        + weight(1) * q_ref[1][:16]
        + weight(2) * next_row(q_y)[:16]
        + weight(3) * q_y[:16]
        + weight(4) * q_z
        + weight(5) * last_col(q_z)
    )
    dens = density[core]
    s_own[...] = -3.0 * dens * dens * (1.0 - young_floor) * energy * (1.0 / GROUP)

    ss_in = [
        send(s_own, s_in.at[n], K_S + n, at(d, b)) for n, (d, b) in enumerate(SPREAD)
    ]
    for c in ss_in:
        c.wait_recv()

    def slab_of(d, b):
        if (d, b) == (0, 0):
            return s_own[...]
        there = slab + b
        ok = jnp.where((there >= 0) & (there < GROUP), 1.0, 0.0).astype(f32)
        return s_in[SPREAD.index((-d, -b))] * (ok * plane_inside(d))

    zeros8 = jnp.zeros((8, NZ), f32)
    fields = {}
    for d in (-1, 0, 1):
        fields[d] = jnp.concatenate(
            [slab_of(d, -1)[8:], slab_of(d, 0), slab_of(d, 1)[:8]], axis=0
        )
    for d in (-2, 2):
        fields[d] = jnp.concatenate([zeros8, slab_of(d, 0), zeros8], axis=0)
    not_first = jnp.where(lane > 0, 1.0, 0.0).astype(f32)

    def smooth(source, middle, above, below):
        beside = (
            above
            + below
            + next_row(middle)
            + last_row(middle)
            + next_col(middle) * not_last
            + last_col(middle) * not_first
        )
        return (source + filter_weight * beside) * (1.0 / (1.0 + 6.0 * filter_weight))

    once = {
        d: smooth(fields[d], fields[d], fields[d + 1], fields[d - 1])
        * (inside * plane_inside(d))
        for d in (-1, 0, 1)
    }
    twice = smooth(fields[0], once[0], once[1], once[-1])
    f_out[rows_here, :] = twice[core]
    outs = [
        send(
            f_out.at[rows_here, :],
            f_out.at[rows_here, :],
            K_OUT + off - 1,
            at(0, off),
        )
        for off in range(1, GROUP)
    ]
    keep.wait()
    for c in xs + outs:
        c.wait_recv()
    for c in sent:
        c.wait_send()


def body(density, fixed_mask, load_mask, load_fields, angle_index):
    angle_rad = angle_index.astype(f32) * (2.0 * math.pi / ANGLES)
    turn = jnp.stack([jnp.cos(angle_rad), jnp.sin(angle_rad)])
    trig = jnp.broadcast_to(turn[:, :, None], (2, 8, 128)).reshape(16, 128)
    vmem = pl.BlockSpec(memory_space=pltpu.VMEM)
    x, filtered = pl.pallas_call(
        kernel,
        out_shape=(
            jax.ShapeDtypeStruct((LOADS, NY, NZ), f32),
            jax.ShapeDtypeStruct((NY, NZ), f32),
        ),
        in_specs=[vmem] * 5,
        out_specs=(pl.BlockSpec(memory_space=pl.ANY), vmem),
        scratch_shapes=[
            pltpu.VMEM((8, 16, 128), f32),
            pltpu.VMEM((5, 32, NZ), f32),
            pltpu.VMEM((2, 16 * 24, 128), f32),
            pltpu.VMEM((20, 16, NZ), f32),
            pltpu.VMEM((2, 18, 16, NZ), f32),
            pltpu.VMEM((20, 16, NZ), f32),
            pltpu.VMEM((2, 18, 16, NZ), f32),
            pltpu.VMEM((16, 32, NZ), f32),
            pltpu.VMEM((18, 16, NZ), f32),
            pltpu.VMEM((18, 16, NZ), f32),
            pltpu.VMEM((2, 16, 16, NZ), f32),
            pltpu.VMEM((4, 16, 128), f32),
            pltpu.VMEM((3, 7, 16, 128), f32),
            pltpu.VMEM((2, 18 * 64, 128), f32),
            pltpu.VMEM((8, 8, 16, NZ), f32),
            pltpu.VMEM((4, 32, NZ), f32),
            pltpu.VMEM((16, NZ), f32),
            pltpu.VMEM((10, 16, NZ), f32),
            pltpu.SemaphoreType.DMA((COPIES,)),
            pltpu.SemaphoreType.DMA((COPIES,)),
            pltpu.SemaphoreType.DMA,
        ],
        compiler_params=pltpu.CompilerParams(
            collective_id=0, has_side_effects=True, vmem_limit_bytes=40 * 2**20
        ),
    )(
        trig,
        density.reshape(NY, NZ),
        fixed_mask.reshape(NY, NZ),
        load_mask.reshape(NY, NZ),
        load_fields.reshape(FIELDS, NY, NZ),
    )
    return x.reshape(1, LOADS, 1, NY, NZ), filtered.reshape(1, NY, NZ)


def solution(mesh):
    in_specs = (
        P("space", None, None),
        P("space", None, None),
        P("space", None, None),
        P(None, None, "space", None, None),
        P("sample"),
    )
    out_specs = (P("sample", None, "space", None, None), P("space", None, None))
    return jax.shard_map(body, mesh=mesh, in_specs=in_specs, out_specs=out_specs, check_vma=False)
```

time: 693 us -> 86.6 us (0.12)
  blocking collectives: 422 us -> 0 us
  waiting for transfers between devices: 158 us -> 0 us
  Pallas kernels: 0 us -> 78.7 us
  starting transfers between devices: 50.6 us -> 0 us
  other arithmetic: 25 us -> 0.07 us
  matrix products: 17.1 us -> 0 us
  between operations: 15.5 us -> 1.44 us
    psum x3 -> x0, blocking collectives: 422 us -> none  [the longest x2 281 us: body(): curv_gram = lax.psum(inner_sum(direction, applied), 'space')]
    psum x1 -> x0, waiting for transfers between devices: 91.9 us -> none  [body(): energy_sum = lax.psum(local_energy, 'sample')]
    pallas_call x0 -> x1, Pallas kernels: none -> 78.7 us  [body(): pl.pallas_call(kernel, out_shape=(jax.ShapeDtypeStruct((LOADS, NY, NZ), f...]
    ppermute x12 -> x0, waiting for transfers between devices: 66.3 us -> none  [the longest x6 45.6 us: extended(): lax.ppermute(head, axis, [((i + 1) % count, i) for i in range(ends)])]
    ppermute x12 -> x0, starting transfers between devices: 50.5 us -> none  [the longest x6 29 us: extended(): lax.ppermute(head, axis, [((i + 1) % count, i) for i in range(ends)])]
    dot_general x8 -> x0, matrix products: 16.1 us -> none  [the longest x4 10.1 us: inner_sum(): jnp.einsum('saxyz,sbxyz->sab', left, right, precision=lax.Precision.HIGHEST)]
    another operation x16 -> x0, other arithmetic: 9.23 us -> none  [the longest x9 4.18 us: block_solve(): factor = jnp.linalg.cholesky(gram_now)]
    concatenate x6 -> x0, other arithmetic: 7.63 us -> none  [extended(): jnp.concatenate([lax.ppermute(tail, axis, [(i, (i + 1) % count) for i in...]
  transfers between devices with their start and end apart: 13 -> 0, of which waited for: 9 -> 0; matrix products, arithmetic and copies ran while one was open for 1% -> 0% of each run, Pallas kernels for 0% -> 0%
where the time goes in v1:
time: 86.6 us; the launch traced here: 86 us
  Pallas kernels  78.7 us (91%)
  local copies, waits for them, and re-layouts  5.79 us (7%)
  between operations  1.44 us (2%)
    pallas_call x1, Pallas kernels, body(): pl.pallas_call(kernel, out_shape=(jax.ShapeDtypeStruct((LOADS, NY, NZ), f...  78.7 us
    unnamed x10, local copies, waits for them, and re-layouts  5.56 us

profile of v1, /device:TPU:1, one launch (start us, length us, event | category | flops | bytes accessed | tf_op | source)
XLA Modules:
  0.0 86.0 jit_solution(14306073984566773911)
XLA Ops:
  1.4 0.1 maximum_bitcast_fusion
  1.5 0.1 broadcast_in_dim.13
  1.6 0.1 broadcast_in_dim.14
  1.7 0.1 broadcast_in_dim.15.trig_in
  1.7 0.0 copy-start
  1.7 1.2 %copy-done = bf16[2,8,1,128,256]{4,3,2,1,0:T(8,128)(2,1)S(1)} copy-done((bf16[2,8,1,128,256]{4,3,2,1,0:T(8,128)(2,1)S(1)}, bf16[2,8,1,128,256]{4,3,2,1,0:T(8,128)(2,1)}, u32[]{:S(2)}) %copy-start) | copy-done | bytes 1048600
  3.0 0.0 copy-start.1
  3.0 0.9 %copy-done.1 = f32[1,128,256]{2,1,0:T(8,128)S(1)} copy-done((f32[1,128,256]{2,1,0:T(8,128)S(1)}, f32[1,128,256]{2,1,0:T(8,128)}, u32[]{:S(2)}) %copy-start.1) | copy-done | bytes 131096
  3.9 0.0 copy-start.2
  3.9 0.9 %copy-done.2 = s32[1,128,256]{2,1,0:T(8,128)S(1)} copy-done((s32[1,128,256]{2,1,0:T(8,128)S(1)}, s32[1,128,256]{2,1,0:T(8,128)}, u32[]{:S(2)}) %copy-start.2) | copy-done | bytes 131096
  4.8 0.0 copy-start.3
  4.8 0.9 %copy-done.3 = s32[1,128,256]{2,1,0:T(8,128)S(1)} copy-done((s32[1,128,256]{2,1,0:T(8,128)S(1)}, s32[1,128,256]{2,1,0:T(8,128)}, u32[]{:S(2)}) %copy-start.3) | copy-done | bytes 131096
  5.7 78.7 %shard_map.68 = (f32[8,128,256]{2,1,0:T(8,128)S(1)}, f32[128,256]{1,0:T(8,128)S(1)}) custom-call(f32[16,128]{1,0:T(8,128)S(1)} %broadcast_in_dim.15.trig_in, f32[128,256]{1,0:T(8,128)S(1)} %bitcast.15, s32[128,256]{1,0:T(8,128)S(1)} %bitcast.16, s32[128,256]{1,0:T(8,128)S(1)} %bitcast.17, bf16[16,128,256]{2,1,0:T(8,128)(2,1)S(1)} %bitcast.12), custom_call_target="tpu_custom_call" | custom-call | tf_op jit(solution)/shard_map/pallas_call | solution.py:577
  84.3 1.0 %copy.11 = f32[1,8,1,128,256]{4,3,2,1,0:T(8,128)} copy(f32[1,8,1,128,256]{4,3,2,1,0:T(8,128)S(1)} %bitcast.13) | data formatting | bytes 2097152
  85.3 0.7 copy.12
Async XLA Ops:
  1.7 1.2 %copy-start = (bf16[2,8,1,128,256]{4,3,2,1,0:T(8,128)(2,1)S(1)}, bf16[2,8,1,128,256]{4,3,2,1,0:T(8,128)(2,1)}, u32[]{:S(2)}) copy-start(bf16[2,8,1,128,256]{4,3,2,1,0:T(8,128)(2,1)} %param.8) | copy-start | bytes 3145732
  3.0 0.9 %copy-start.1 = (f32[1,128,256]{2,1,0:T(8,128)S(1)}, f32[1,128,256]{2,1,0:T(8,128)}, u32[]{:S(2)}) copy-start(f32[1,128,256]{2,1,0:T(8,128)} %param.5) | copy-start | bytes 393220
  3.9 0.9 %copy-start.2 = (s32[1,128,256]{2,1,0:T(8,128)S(1)}, s32[1,128,256]{2,1,0:T(8,128)}, u32[]{:S(2)}) copy-start(s32[1,128,256]{2,1,0:T(8,128)} %param.6) | copy-start | bytes 393220
  4.8 0.9 %copy-start.3 = (s32[1,128,256]{2,1,0:T(8,128)S(1)}, s32[1,128,256]{2,1,0:T(8,128)}, u32[]{:S(2)}) copy-start(s32[1,128,256]{2,1,0:T(8,128)} %param.7) | copy-start | bytes 393220

commit v2 on v1

--- a/solution.py
+++ b/solution.py
@@ -25,12 +25,13 @@
 K_TRIG = 0
 K_MOD = 7
 K_F = 11
-K_V = 13
-K_GRAM = 15
-K_X = 36
-K_S = 43
-K_OUT = 53
-COPIES = 60
+K_V = 15
+K_GRAM = 19
+K_MIXED = 44
+K_S = 51
+K_OUT = 61
+K_SCALE = 68
+COPIES = 75
 
 SPREAD = [(d, e) for d in (-1, 0, 1) for e in (-1, 0, 1) if (d, e) != (0, 0)] + [
     (-2, 0),
@@ -121,6 +122,18 @@
     load_ref,
     x_out,
     f_out,
+    den_in,
+    fix_in,
+    mask_in,
+    load_in,
+    load_all,
+    scale_all,
+    z_all,
+    v_all,
+    x_all,
+    v_send,
+    v_half,
+    factors,
     trig,
     mod,
     dense,
@@ -135,24 +148,25 @@
     gram,
     gram_in,
     x_own,
-    x_send,
     q_ref,
     s_own,
     s_in,
     send_sem,
     recv_sem,
+    fetch_sem,
     local_sem,
 ):
     plane = lax.axis_index("space")
     slab = lax.axis_index("sample")
     zpos = plane // GROUP
     ypos = plane % GROUP
+    other_core = (plane // 2) * 2 + (plane + 1) % 2
 
     def at(planes, slabs):
         return ((plane + PLANES + planes) % PLANES, (slab + GROUP + slabs) % GROUP)
 
     def y_mate(off):
-        return (zpos * GROUP + (ypos + off) % GROUP, slab)
+        return (zpos * GROUP + (ypos + 2 * off) % GROUP, slab)
 
     def z_mate(off):
         return (((zpos + off) % GROUP) * GROUP + ypos, slab)
@@ -167,56 +181,62 @@
             device_id_type=MESH,
         )
 
-    mates = [at(0, off) for off in range(1, GROUP)]
-    mates += [at(d, 0) for d in (-2, -1, 1, 2)]
+    mates = [at(d, 0) for d in (-1, 1, -2, 2)]
+    mates += [at(0, off) for off in range(1, GROUP)]
     mates += [at(d, e) for d in (-1, 1) for e in (-1, 1)]
-    mates += [y_mate(off) for off in range(1, GROUP)]
-    mates += [z_mate(off) for off in range(1, GROUP)]
+    near = [(other_core, (slab + off) % GROUP) for off in range(GROUP)]
+    stages = [
+        [z_mate(off) for off in range(1, GROUP)],
+        [y_mate(off) for off in range(1, 4)],
+        [at(0, off) for off in range(1, GROUP)] + near,
+    ]
+    mates += stages[0] + stages[1] + near
     barrier = pltpu.get_barrier_semaphore()
     for mate in mates:
         pl.semaphore_signal(barrier, inc=1, device_id=mate, device_id_type=MESH)
 
-    before = pl.multiple_of(((slab + GROUP - 1) % GROUP) * SLAB, SLAB)
+    fetches = []
+    for n in range(3):
+        rows = pl.ds(pl.multiple_of(((slab + GROUP - 1 + n) % GROUP) * SLAB, SLAB), SLAB)
+        put = pl.ds(n * SLAB, SLAB)
+        for k, (src, dst) in enumerate(
+            (
+                (den_ref.at[rows], den_in.at[put]),
+                (fix_ref.at[rows], fix_in.at[put]),
+                (mask_ref.at[rows], mask_in.at[put]),
+                (load_ref.at[:, rows], load_in.at[:, put]),
+            )
+        ):
+            fetches.append(pltpu.make_async_copy(src, dst, fetch_sem.at[4 * n + k]))
+    whole = pltpu.make_async_copy(load_ref, load_all, fetch_sem.at[12])
+    for c in fetches + [whole]:
+        c.start()
     here = pl.multiple_of(slab * SLAB, SLAB)
-    after = pl.multiple_of(((slab + 1) % GROUP) * SLAB, SLAB)
 
     def window(ref):
-        return jnp.concatenate(
-            [
-                ref[pl.ds(before, SLAB), :][8:],
-                ref[pl.ds(here, SLAB), :],
-                ref[pl.ds(after, SLAB), :][:8],
-            ],
-            axis=0,
-        )
+        return ref[8:40, :]
 
     row = lax.broadcasted_iota(jnp.int32, (32, NZ), 0) + (slab * SLAB - 8)
     inside = jnp.where((row >= 0) & (row < NY), 1.0, 0.0).astype(f32)
     lane = lax.broadcasted_iota(jnp.int32, (32, NZ), 1)
     not_last = jnp.where(lane < NZ - 1, 1.0, 0.0).astype(f32)
-    density = window(den_ref)
-    free = inside * (1.0 - window(fix_ref).astype(f32))
-    loaded = free * window(mask_ref).astype(f32)
+    for c in fetches:
+        c.wait()
+    density = window(den_in)
+    free = inside * (1.0 - window(fix_in).astype(f32))
+    loaded = free * window(mask_in).astype(f32)
     modulus = inside * (young_floor + (1.0 - young_floor) * density * density * density)
     mod[2] = modulus
     trig[0] = trig_in[...]
 
     for k in range(FIELDS):
-        rows = jnp.concatenate(
-            [
-                load_ref[k, pl.ds(before, SLAB), :].astype(f32)[12:],
-                load_ref[k, pl.ds(here, SLAB), :].astype(f32),
-                load_ref[k, pl.ds(after, SLAB), :].astype(f32)[:4],
-            ],
-            axis=0,
-        )
-        rows = rows * loaded[4:28]
-        dense[0, 24 * k : 24 * k + 24, :] = rows[:, :128]
-        dense[1, 24 * k : 24 * k + 24, :] = rows[:, 128:]
+        rows = load_in[k].astype(f32)[8:40] * loaded
+        dense[0, 32 * k : 32 * k + 32, :] = rows[:, :128]
+        dense[1, 32 * k : 32 * k + 32, :] = rows[:, 128:]
     for r in range(20):
         for h in range(2):
             f_own[r, :, 128 * h : 128 * h + 128] = dense[
-                h, pl.ds(r + 2, FIELDS, stride=24), :
+                h, pl.ds(r + 6, FIELDS, stride=32), :
             ]
 
     pl.semaphore_wait(barrier, len(mates))
@@ -233,10 +253,13 @@
         send(mod.at[2], mod.at[2 - d], K_MOD + n, at(d, 0))
         for n, d in enumerate((-2, -1, 1, 2))
     ]
-    fs = [
-        send(f_own.at[pl.ds(1, 18)], f_rim.at[0], K_F, at(-1, 0)),
-        send(f_own.at[pl.ds(1, 18)], f_rim.at[1], K_F + 1, at(1, 0)),
-    ]
+    fs = []
+    for half in range(2):
+        src, dst = pl.ds(1 + 9 * half, 9), pl.ds(9 * half, 9)
+        for n, d in enumerate((-1, 1)):
+            fs.append(
+                send(f_own.at[src], f_rim.at[n, dst], K_F + 2 * half + n, at(d, 0))
+            )
     trigs = [
         send(trig.at[0], trig.at[off], K_TRIG + off - 1, at(0, off))
         for off in range(1, GROUP)
@@ -278,6 +301,18 @@
     coef[7] = rim_inverse(m_up, harmonic(m_up, m_up2), up)
     coef[8] = rim_inverse(m_dn, harmonic(m_dn, m_dn2), down)
 
+    rows_here = pl.ds(here, SLAB)
+    scale_all[rows_here, :] = (loaded * inverse)[8:24]
+    scales = [
+        send(
+            scale_all.at[rows_here],
+            scale_all.at[rows_here],
+            K_SCALE + off - 1,
+            at(0, off),
+        )
+        for off in range(1, GROUP)
+    ]
+
     def along(n, w):
         return coef[n, pl.ds(w, 1), :]
 
@@ -285,70 +320,112 @@
     def _(r):
         z_own[r] = f_own[r] * along(6, r + 6)
 
-    for c in fs:
+    def send_v(first, n, k):
+        rows = pl.ds(first, 8)
+        return send(
+            v_own.at[pl.ds(first + 1, 8)], v_rim.at[n, rows], K_V + k, at(2 * n - 1, 0)
+        )
+
+    vs = []
+    for half in range(2):
+        for c in fs[2 * half : 2 * half + 2]:
+            c.wait_recv()
+
+        @pl.loop(9 * half, 9 * half + 9)
+        def _(r):
+            w = r + 7
+            z = z_own[r + 1]
+            z_up = f_rim[0, r] * along(7, w)
+            z_down = f_rim[1, r] * along(8, w)
+            z_rim[0, r] = z_up
+            z_rim[1, r] = z_down
+            image = (
+                along(0, w) * z_up
+                + along(1, w) * z_down
+                + along(2, w) * z_own[r + 2]
+                + along(3, w) * z_own[r]
+                + along(4, w) * next_col(z)
+                + along(5, w) * last_col(z)
+            )
+            e_own[r] = image
+            v = image * along(6, w)
+            v_own[r] = v
+            for h in range(2):
+                v_half[h, pl.ds(pl.multiple_of(r * FIELDS, FIELDS), FIELDS), :] = v[
+                    :, 128 * h : 128 * h + 128
+                ]
+
+        vs.append(send_v(8 * half, 1 - half, half))
+    late_vs = [send_v(8, 1, 2), send_v(0, 0, 3)]
+
+    for c in trigs:
         c.wait_recv()
-
-    @pl.loop(0, 18)
-    def _(r):
-        z_rim[0, r] = f_rim[0, r] * along(7, r + 7)
-        z_rim[1, r] = f_rim[1, r] * along(8, r + 7)
-
-    @pl.loop(0, 18)
-    def _(r):
-        w = r + 7
-        z = z_own[r + 1]
-        image = (
-            along(0, w) * z_rim[0, r]
-            + along(1, w) * z_rim[1, r]
-            + along(2, w) * z_own[r + 2]
-            + along(3, w) * z_own[r]
-            + along(4, w) * next_col(z)
-            + along(5, w) * last_col(z)
-        )
-        e_own[r] = image
-        v_own[r] = image * along(6, w)
-
-    vs = [
-        send(v_own.at[pl.ds(1, 16)], v_rim.at[0], K_V, at(-1, 0)),
-        send(v_own.at[pl.ds(1, 16)], v_rim.at[1], K_V + 1, at(1, 0)),
+    for b in range(LOADS):
+        for h in range(2):
+            cols = slice(128 * h, 128 * h + 128)
+            v_x = v_half[h, pl.ds(FIELDS + b, SLAB, stride=FIELDS), :]
+            v_y = v_half[h, pl.ds(FIELDS + LOADS + b, SLAB, stride=FIELDS), :]
+            for off in range(GROUP):
+                turn = trig[(GROUP - off) % GROUP]
+                mixed = turn[0:1] * v_x + turn[8:9] * v_y
+                if off == 0:
+                    v_all[b, rows_here, cols] = mixed
+                else:
+                    v_send[off, b, :, cols] = mixed
+
+    mixed_vs = [
+        send(
+            v_send.at[off],
+            v_all.at[:, rows_here, :],
+            K_MIXED + off - 1,
+            at(0, off),
+        )
+        for off in (2, 6, 4)
     ]
-
     contract = (((1,), (1,)), ((), ()))
 
     def first_gram(c, acc):
-        zh, zl = split(z_own[c + 2])
-        vh, vl = split(v_own[c + 1])
-        fh, fl = split(f_own[c + 2])
-        eh, el = split(e_own[c + 1])
-        left = jnp.concatenate([zh, vh, zl, vl], axis=0)
-        right = jnp.concatenate([fh, eh, fl, el, fh, eh, fl, el], axis=0)
-        return acc + lax.dot_general(left, right, contract, preferred_element_type=f32)
-
-    acc = lax.fori_loop(0, SLAB, first_gram, jnp.zeros((64, 128), f32))
-    acc = acc[:32] + acc[32:]
-    acc = acc + pltpu.roll(acc, 128 - 32, 1)
-
-    for c in vs:
-        c.wait_recv()
-
-    def second_gram(c, acc):
         w = c + 8
         v = v_own[c + 1]
-        image = (
-            along(0, w) * v_rim[0, c]
-            + along(1, w) * v_rim[1, c]
-            + along(2, w) * v_own[c + 2]
+        flat = (
+            along(2, w) * v_own[c + 2]
             + along(3, w) * v_own[c]
             + along(4, w) * next_col(v)
             + along(5, w) * last_col(v)
         )
+        zh, zl = split(z_own[c + 2])
         vh, vl = split(v)
-        nh, nl = split(image)
-        left = jnp.concatenate([vh, vl], axis=0)
-        right = jnp.concatenate([nh, nl, nh, nl, nh, nl, nh, nl], axis=0)
+        fh, fl = split(f_own[c + 2])
+        eh, el = split(e_own[c + 1])
+        nh, nl = split(flat)
+        left = jnp.concatenate([zh, vh, zl, vl], axis=0)
+        right = jnp.concatenate([fh, eh, fl, el, nh, nl, nh, nl], axis=0)
         return acc + lax.dot_general(left, right, contract, preferred_element_type=f32)
 
-    acc2 = lax.fori_loop(0, SLAB, second_gram, jnp.zeros((32, 128), f32))
+    acc = lax.fori_loop(0, SLAB, first_gram, jnp.zeros((64, 128), f32))
+    acc = acc[:32] + acc[32:]
+    flat_part = acc[16:]
+    flat_part = flat_part + pltpu.roll(flat_part, 128 - 16, 1)
+    acc = acc + pltpu.roll(acc, 128 - 32, 1)
+
+    def second_gram(n, coef_n):
+        def step(c, acc):
+            vh, vl = split(v_own[c + 1])
+            wh, wl = split(along(coef_n, c + 8) * v_rim[n, c])
+            left = jnp.concatenate([vh, vl, wh, wl], axis=0)
+            right = jnp.concatenate([wh, wl, vh, vl, wh, wl, vh, vl], axis=0)
+            return acc + lax.dot_general(
+                left, right, contract, preferred_element_type=f32
+            )
+
+        return step
+
+    acc2 = jnp.zeros((64, 128), f32)
+    vs[0].wait_recv()
+    acc2 = lax.fori_loop(0, 8, second_gram(1, 1), acc2)
+    vs[1].wait_recv()
+    acc2 = lax.fori_loop(8, 16, second_gram(0, 0), acc2)
+    acc2 = acc2[:32] + pltpu.roll(acc2[32:], 128 - 32, 1)
     acc2 = acc2[:16] + acc2[16:]
     acc2 = acc2 + pltpu.roll(acc2, 128 - 16, 1)
 
@@ -359,27 +436,60 @@
         jnp.where(
             wide < 48,
             pltpu.roll(acc[16:], 16, 1),
-            jnp.where(wide < 64, pltpu.roll(acc2, 48, 1), 0.0),
+            jnp.where(
+                wide < 64,
+                pltpu.roll(acc2, 48, 1) + pltpu.roll(flat_part, 128 - 16, 1),
+                0.0,
+            ),
         ),
     )
-    for stage, mate in enumerate((lambda off: at(0, off), y_mate, z_mate)):
+    first = 0
+    for stage, group in enumerate(stages):
         gram[stage] = packed
         arriving = [
-            send(
-                gram.at[stage],
-                gram_in.at[stage, off - 1],
-                K_GRAM + 7 * stage + off - 1,
-                mate(off),
-            )
-            for off in range(1, GROUP)
+            send(gram.at[stage], gram_in.at[first + n], K_GRAM + first + n, mate)
+            for n, mate in enumerate(group)
         ]
+        if stage == 0:
+            whole.wait()
+            for c in scales:
+                c.wait_recv()
+
+            @pl.loop(0, GROUP)
+            def _(j):
+                rows = pl.ds(pl.multiple_of(j * SLAB, SLAB), SLAB)
+                by_x = scale_all[rows, :] * jnp.concatenate([trig[0, 0:1]] * 2, axis=1)
+                by_y = scale_all[rows, :] * jnp.concatenate([trig[0, 8:9]] * 2, axis=1)
+                for b in range(LOADS):
+                    z_all[b, rows, :] = by_x * load_all[b, rows, :].astype(
+                        f32
+                    ) + by_y * load_all[LOADS + b, rows, :].astype(f32)
+
+        if stage == 0:
+            mixed_vs += [
+                send(
+                    v_send.at[off],
+                    v_all.at[:, rows_here, :],
+                    K_MIXED + off - 1,
+                    at(0, off),
+                )
+                for off in (1, 7)
+            ]
         for n, c in enumerate(arriving):
             c.wait_recv()
-            packed = packed + gram_in[stage, n]
-
+            packed = packed + gram_in[first + n]
+        first += len(group)
+
+    mixed_vs += [
+        send(
+            v_send.at[off],
+            v_all.at[:, rows_here, :],
+            K_MIXED + off - 1,
+            at(0, off),
+        )
+        for off in (3, 5)
+    ]
     narrow = lax.broadcasted_iota(jnp.int32, (8, 128), 1)
-    for c in trigs:
-        c.wait_recv()
     cosine = jnp.zeros((8, 128), f32)
     sine = jnp.zeros((8, 128), f32)
     for off in range(GROUP):
@@ -453,25 +563,8 @@
                 :, 128 * h : 128 * h + 128
             ]
 
-    for s in range(GROUP):
-        for b in range(LOADS):
-            for h in range(2):
-                x_send[s, b, :, 128 * h : 128 * h + 128] = x_own[
-                    h, pl.ds(64 + 8 * s + b, SLAB, stride=64), :
-                ]
-
-    rows_here = pl.ds(here, SLAB)
-    keep = pltpu.make_async_copy(x_send.at[slab], x_out.at[:, rows_here, :], local_sem)
-    keep.start()
-    xs = [
-        send(
-            x_send.at[(slab + off) % GROUP],
-            x_out.at[:, rows_here, :],
-            K_X + off - 1,
-            at(0, off),
-        )
-        for off in range(1, GROUP)
-    ]
+    for c in late_vs:
+        c.wait_recv()
 
     def squares(a, b):
         d = a - b
@@ -515,6 +608,30 @@
     ss_in = [
         send(s_own, s_in.at[n], K_S + n, at(d, b)) for n, (d, b) in enumerate(SPREAD)
     ]
+    for a in range(LOADS):
+        for part, rows in ((0, on_z), (1, on_v)):
+            mine = jnp.where(narrow == slab, rows[a], 0.0)
+            mine = jnp.broadcast_to(jnp.sum(mine, axis=1, keepdims=True), (8, 128))
+            for b in range(LOADS):
+                factors[(part * LOADS + a) * LOADS + b] = spread_row(mine, b)
+    for c in mixed_vs:
+        c.wait_recv()
+
+    @pl.loop(0, NY // 8)
+    def _(j):
+        rows = pl.ds(pl.multiple_of(j * 8, 8), 8)
+        for h in range(2):
+            cols = slice(128 * h, 128 * h + 128)
+            basis = [z_all[a, rows, cols] for a in range(LOADS)]
+            basis += [v_all[a, rows, cols] for a in range(LOADS)]
+            for b in range(LOADS):
+                total = factors[b] * basis[0]
+                for a in range(1, 2 * LOADS):
+                    total = total + factors[a * LOADS + b] * basis[a]
+                x_all[b, rows, cols] = total
+
+    keep = pltpu.make_async_copy(x_all, x_out, local_sem)
+    keep.start()
     for c in ss_in:
         c.wait_recv()
 
@@ -563,7 +680,7 @@
         for off in range(1, GROUP)
     ]
     keep.wait()
-    for c in xs + outs:
+    for c in outs:
         c.wait_recv()
     for c in sent:
         c.wait_send()
@@ -580,12 +697,24 @@
             jax.ShapeDtypeStruct((LOADS, NY, NZ), f32),
             jax.ShapeDtypeStruct((NY, NZ), f32),
         ),
-        in_specs=[vmem] * 5,
+        in_specs=[vmem] + [pl.BlockSpec(memory_space=pltpu.HBM)] * 4,
         out_specs=(pl.BlockSpec(memory_space=pl.ANY), vmem),
         scratch_shapes=[
+            pltpu.VMEM((48, NZ), f32),
+            pltpu.VMEM((48, NZ), jnp.int32),
+            pltpu.VMEM((48, NZ), jnp.int32),
+            pltpu.VMEM((FIELDS, 48, NZ), bf16),
+            pltpu.VMEM((FIELDS, NY, NZ), bf16),
+            pltpu.VMEM((NY, NZ), f32),
+            pltpu.VMEM((LOADS, NY, NZ), f32),
+            pltpu.VMEM((LOADS, NY, NZ), f32),
+            pltpu.VMEM((LOADS, NY, NZ), f32),
+            pltpu.VMEM((GROUP, LOADS, SLAB, NZ), f32),
+            pltpu.VMEM((2, 18 * FIELDS, 128), f32),
+            pltpu.VMEM((2 * LOADS * LOADS, 8, 128), f32),
             pltpu.VMEM((8, 16, 128), f32),
             pltpu.VMEM((5, 32, NZ), f32),
-            pltpu.VMEM((2, 16 * 24, 128), f32),
+            pltpu.VMEM((2, 16 * 32, 128), f32),
             pltpu.VMEM((20, 16, NZ), f32),
             pltpu.VMEM((2, 18, 16, NZ), f32),
             pltpu.VMEM((20, 16, NZ), f32),
@@ -594,19 +723,19 @@
             pltpu.VMEM((18, 16, NZ), f32),
             pltpu.VMEM((18, 16, NZ), f32),
             pltpu.VMEM((2, 16, 16, NZ), f32),
-            pltpu.VMEM((4, 16, 128), f32),
-            pltpu.VMEM((3, 7, 16, 128), f32),
+            pltpu.VMEM((3, 16, 128), f32),
+            pltpu.VMEM((25, 16, 128), f32),
             pltpu.VMEM((2, 18 * 64, 128), f32),
-            pltpu.VMEM((8, 8, 16, NZ), f32),
             pltpu.VMEM((4, 32, NZ), f32),
             pltpu.VMEM((16, NZ), f32),
             pltpu.VMEM((10, 16, NZ), f32),
             pltpu.SemaphoreType.DMA((COPIES,)),
             pltpu.SemaphoreType.DMA((COPIES,)),
+            pltpu.SemaphoreType.DMA((13,)),
             pltpu.SemaphoreType.DMA,
         ],
         compiler_params=pltpu.CompilerParams(
-            collective_id=0, has_side_effects=True, vmem_limit_bytes=40 * 2**20
+            collective_id=0, has_side_effects=True, vmem_limit_bytes=64 * 2**20
         ),
     )(
         trig,

time: 86.6 us -> 74.6 us (0.86)
  Pallas kernels: 78.7 us -> 69 us
  local copies, waits for them, and re-layouts: 5.79 us -> 3.79 us
    pallas_call x1, Pallas kernels: 78.7 us -> 69 us  [body(): pl.pallas_call(kernel, out_shape=(jax.ShapeDtypeStruct((LOADS, NY, NZ), f...]
    unnamed x10 -> x4, local copies, waits for them, and re-layouts: 5.56 us -> 2.96 us
where the time goes in v2:
time: 74.6 us; the launch traced here: 74.3 us
  Pallas kernels  69 us (92%)
  local copies, waits for them, and re-layouts  3.79 us (5%)
  between operations  1.45 us (2%)
    pallas_call x1, Pallas kernels, body(): pl.pallas_call(kernel, out_shape=(jax.ShapeDtypeStruct((LOADS, NY, NZ), f...  69 us
    unnamed x4, local copies, waits for them, and re-layouts  2.96 us

profile of v2, /device:TPU:1, one launch (start us, length us, event | category | flops | bytes accessed | tf_op | source)
XLA Modules:
  0.0 74.3 jit_solution(8130731213081043811)
XLA Ops:
  1.4 0.1 maximum_bitcast_fusion
  1.5 0.1 broadcast_in_dim.13
  1.6 0.1 broadcast_in_dim.14
  1.7 0.7 broadcast_in_dim.15.trig_in
  2.3 69.0 %shard_map.68 = (f32[8,128,256]{2,1,0:T(8,128)}, f32[128,256]{1,0:T(8,128)}) custom-call(f32[16,128]{1,0:T(8,128)} %broadcast_in_dim.15.trig_in, f32[128,256]{1,0:T(8,128)} %bitcast.15, s32[128,256]{1,0:T(8,128)} %bitcast.16, s32[128,256]{1,0:T(8,128)} %bitcast.17, bf16[16,128,256]{2,1,0:T(8,128)(2,1)} %bitcast.12), custom_call_target="tpu_custom_call" | custom-call | tf_op jit(solution)/shard_map/pallas_call | solution.py:694
  71.3 0.0 copy-start
  71.3 2.3 %copy.11 = f32[1,8,1,128,256]{4,3,2,1,0:T(8,128)} copy(f32[1,8,1,128,256]{4,3,2,1,0:T(8,128)} %bitcast.13) | data formatting | bytes 2097152
  73.6 0.0 copy-done
  73.6 0.7 copy.12
Async XLA Ops:
  71.3 2.3 %copy-start = (f32[128,256]{1,0:T(8,128)S(1)}, f32[128,256]{1,0:T(8,128)}, u32[]{:S(2)}) copy-start(f32[128,256]{1,0:T(8,128)} %get-tuple-element.5) | copy-start | bytes 393220

commit v3 on v2

--- a/solution.py
+++ b/solution.py
@@ -33,10 +33,8 @@
 K_SCALE = 68
 COPIES = 75
 
-SPREAD = [(d, e) for d in (-1, 0, 1) for e in (-1, 0, 1) if (d, e) != (0, 0)] + [
-    (-2, 0),
-    (2, 0),
-]
+SPREAD = [(-2, 0), (2, 0), (-1, -1), (1, 1), (-1, 1), (1, -1)]
+SPREAD += [(-1, 0), (1, 0), (0, -1), (0, 1)]
 
 
 def harmonic(a, b):
@@ -115,7 +113,7 @@
 
 
 def kernel(
-    trig_in,
+    angle_ref,
     den_ref,
     fix_ref,
     mask_ref,
@@ -186,9 +184,9 @@
     mates += [at(d, e) for d in (-1, 1) for e in (-1, 1)]
     near = [(other_core, (slab + off) % GROUP) for off in range(GROUP)]
     stages = [
-        [z_mate(off) for off in range(1, GROUP)],
-        [y_mate(off) for off in range(1, 4)],
-        [at(0, off) for off in range(1, GROUP)] + near,
+        [z_mate(off) for off in (4, 3, 5, 2, 6, 1, 7)],
+        [y_mate(off) for off in (2, 1, 3)],
+        near[3:6] + [at(0, off) for off in (4, 3, 5, 2, 6, 1, 7)] + near[6:] + near[:3],
     ]
     mates += stages[0] + stages[1] + near
     barrier = pltpu.get_barrier_semaphore()
@@ -227,7 +225,10 @@
     loaded = free * window(mask_in).astype(f32)
     modulus = inside * (young_floor + (1.0 - young_floor) * density * density * density)
     mod[2] = modulus
-    trig[0] = trig_in[...]
+    turned = jnp.full((8, 128), angle_ref[0], jnp.int32).astype(f32)
+    turned = turned * (2.0 * math.pi / ANGLES)
+    trig[0, :8, :] = jnp.cos(turned)
+    trig[0, 8:, :] = jnp.sin(turned)
 
     for k in range(FIELDS):
         rows = load_in[k].astype(f32)[8:40] * loaded
@@ -303,16 +304,6 @@
 
     rows_here = pl.ds(here, SLAB)
     scale_all[rows_here, :] = (loaded * inverse)[8:24]
-    scales = [
-        send(
-            scale_all.at[rows_here],
-            scale_all.at[rows_here],
-            K_SCALE + off - 1,
-            at(0, off),
-        )
-        for off in range(1, GROUP)
-    ]
-
     def along(n, w):
         return coef[n, pl.ds(w, 1), :]
 
@@ -357,6 +348,15 @@
 
         vs.append(send_v(8 * half, 1 - half, half))
     late_vs = [send_v(8, 1, 2), send_v(0, 0, 3)]
+    scales = [
+        send(
+            scale_all.at[rows_here],
+            scale_all.at[rows_here],
+            K_SCALE + off - 1,
+            at(0, off),
+        )
+        for off in range(1, GROUP)
+    ]
 
     for c in trigs:
         c.wait_recv()
@@ -384,7 +384,7 @@
     ]
     contract = (((1,), (1,)), ((), ()))
 
-    def first_gram(c, acc):
+    def first_parts(c):
         w = c + 8
         v = v_own[c + 1]
         flat = (
@@ -400,31 +400,37 @@
         nh, nl = split(flat)
         left = jnp.concatenate([zh, vh, zl, vl], axis=0)
         right = jnp.concatenate([fh, eh, fl, el, nh, nl, nh, nl], axis=0)
-        return acc + lax.dot_general(left, right, contract, preferred_element_type=f32)
-
-    acc = lax.fori_loop(0, SLAB, first_gram, jnp.zeros((64, 128), f32))
+        return left, right
+
+    def second_parts(n, coef_n):
+        def parts(c):
+            vh, vl = split(v_own[c + 1])
+            wh, wl = split(along(coef_n, c + 8) * v_rim[n, c])
+            left = jnp.concatenate([vh, vl, wh, wl], axis=0)
+            right = jnp.concatenate([wh, wl, vh, vl, wh, wl, vh, vl], axis=0)
+            return left, right
+
+        return parts
+
+    def gram_of(parts, rows):
+        both = [parts(c) for c in rows]
+        left = jnp.concatenate([one for one, _ in both], axis=1)
+        right = jnp.concatenate([one for _, one in both], axis=1)
+        return lax.dot_general(left, right, contract, preferred_element_type=f32)
+
+    def four_rows(j, acc):
+        return acc + gram_of(first_parts, [4 * j + t for t in range(4)])
+
+    acc = lax.fori_loop(0, SLAB // 4, four_rows, jnp.zeros((64, 128), f32))
     acc = acc[:32] + acc[32:]
     flat_part = acc[16:]
     flat_part = flat_part + pltpu.roll(flat_part, 128 - 16, 1)
     acc = acc + pltpu.roll(acc, 128 - 32, 1)
 
-    def second_gram(n, coef_n):
-        def step(c, acc):
-            vh, vl = split(v_own[c + 1])
-            wh, wl = split(along(coef_n, c + 8) * v_rim[n, c])
-            left = jnp.concatenate([vh, vl, wh, wl], axis=0)
-            right = jnp.concatenate([wh, wl, vh, vl, wh, wl, vh, vl], axis=0)
-            return acc + lax.dot_general(
-                left, right, contract, preferred_element_type=f32
-            )
-
-        return step
-
-    acc2 = jnp.zeros((64, 128), f32)
     vs[0].wait_recv()
-    acc2 = lax.fori_loop(0, 8, second_gram(1, 1), acc2)
+    acc2 = gram_of(second_parts(1, 1), range(8))
     vs[1].wait_recv()
-    acc2 = lax.fori_loop(8, 16, second_gram(0, 0), acc2)
+    acc2 = acc2 + gram_of(second_parts(0, 0), range(8, 16))
     acc2 = acc2[:32] + pltpu.roll(acc2[32:], 128 - 32, 1)
     acc2 = acc2[:16] + acc2[16:]
     acc2 = acc2 + pltpu.roll(acc2, 128 - 16, 1)
@@ -443,6 +449,7 @@
             ),
         ),
     )
+    packed = jnp.where(wide[:8] < 64, packed[:8], pltpu.roll(packed[8:], 64, 1))
     first = 0
     for stage, group in enumerate(stages):
         gram[stage] = packed
@@ -489,6 +496,8 @@
         )
         for off in (3, 5)
     ]
+    packed = jnp.concatenate([packed, pltpu.roll(packed, 64, 1)], axis=0)
+
     narrow = lax.broadcasted_iota(jnp.int32, (8, 128), 1)
     cosine = jnp.zeros((8, 128), f32)
     sine = jnp.zeros((8, 128), f32)
@@ -512,14 +521,16 @@
 
     g0, sm, ym, tm = matrix(0), matrix(16), matrix(32), matrix(48)
     cm = minus(g0, sm)
+    level = lax.broadcasted_iota(jnp.int32, (8, 128), 0)
+    unit = [jnp.where(level == i, 1.0, 0.0).astype(f32) for i in range(LOADS)]
+    g0_inverse = solve(g0, unit)
     e = solve(cm, sm)
-    level = lax.broadcasted_iota(jnp.int32, (8, 128), 0)
-    p = [e[i] + jnp.where(level == i, 1.0, 0.0).astype(f32) for i in range(LOADS)]
+    p = plus(e, unit)
     g1 = minus(
         product_t(p, minus(product(ym, p), product(sm, e))),
         product_t(e, minus(product(sm, p), product(g0, e))),
     )
-    q = minus(solve(g0, g1), e)
+    q = minus(product(g0_inverse, g1), e)
     smy = minus(sm, ym)
     curv = plus(
         product_t(q, plus(product(cm, q), product(smy, p))),
@@ -555,13 +566,15 @@
         basis = jnp.concatenate([zh, vh, zl, vl, zh, vh, zl, vl], axis=0)
         return jnp.dot(mix, basis, preferred_element_type=f32)
 
-    @pl.loop(0, 18)
-    def _(r):
-        x = iterates(z_own[r + 1], v_own[r])
-        for h in range(2):
-            x_own[h, pl.ds(pl.multiple_of(r * 64, 64), 64), :] = x[
-                :, 128 * h : 128 * h + 128
-            ]
+    @pl.loop(0, 6)
+    def _(j):
+        for t in range(3):
+            r = 3 * j + t
+            x = iterates(z_own[r + 1], v_own[r])
+            for h in range(2):
+                x_own[h, pl.ds(pl.multiple_of(r * 64, 64), 64), :] = x[
+                    :, 128 * h : 128 * h + 128
+                ]
 
     for c in late_vs:
         c.wait_recv()
@@ -574,16 +587,19 @@
         rows = pl.ds(pl.multiple_of(r * 64, 64), 64)
         return jnp.concatenate([x_own[0, rows, :], x_own[1, rows, :]], axis=1)
 
-    @pl.loop(0, 17)
-    def _(r):
-        q_ref[2, pl.ds(r, 1), :] = squares(x_row(r), x_row(r + 1))
-
-    @pl.loop(0, 16)
-    def _(c):
-        x = x_row(c + 1)
-        q_ref[0, pl.ds(c, 1), :] = squares(x, iterates(z_rim[0, c + 1], v_rim[0, c]))
-        q_ref[1, pl.ds(c, 1), :] = squares(x, iterates(z_rim[1, c + 1], v_rim[1, c]))
-        q_ref[3, pl.ds(c, 1), :] = squares(x, next_col(x))
+    q_ref[2, 0:1, :] = squares(x_row(0), x_row(1))
+
+    @pl.loop(0, 8)
+    def _(j):
+        for t in range(2):
+            c = 2 * j + t
+            x = x_row(c + 1)
+            x_up = iterates(z_rim[0, c + 1], v_rim[0, c])
+            x_down = iterates(z_rim[1, c + 1], v_rim[1, c])
+            q_ref[0, pl.ds(c, 1), :] = squares(x, x_up)
+            q_ref[1, pl.ds(c, 1), :] = squares(x, x_down)
+            q_ref[2, pl.ds(c + 1, 1), :] = squares(x, x_row(c + 2))
+            q_ref[3, pl.ds(c, 1), :] = squares(x, next_col(x))
 
     core = slice(8, 24)
     softness = 1.0 / m0[core]
@@ -686,10 +702,27 @@
         c.wait_send()
 
 
+def hand_on(x_ref, f_ref, x_out, f_out, x_part, f_part, sems_in, sems_out):
+    ways = [(x_ref.at[b], x_part.at[b], x_out.at[b]) for b in range(LOADS)]
+    ways.append((f_ref, f_part, f_out))
+    arriving = [
+        pltpu.make_async_copy(src, part, sems_in.at[n])
+        for n, (src, part, _) in enumerate(ways)
+    ]
+    leaving = [
+        pltpu.make_async_copy(part, dst, sems_out.at[n])
+        for n, (_, part, dst) in enumerate(ways)
+    ]
+    for c in arriving:
+        c.start()
+    for before, c in zip(arriving, leaving):
+        before.wait()
+        c.start()
+    for c in leaving:
+        c.wait()
+
+
 def body(density, fixed_mask, load_mask, load_fields, angle_index):
-    angle_rad = angle_index.astype(f32) * (2.0 * math.pi / ANGLES)
-    turn = jnp.stack([jnp.cos(angle_rad), jnp.sin(angle_rad)])
-    trig = jnp.broadcast_to(turn[:, :, None], (2, 8, 128)).reshape(16, 128)
     vmem = pl.BlockSpec(memory_space=pltpu.VMEM)
     x, filtered = pl.pallas_call(
         kernel,
@@ -697,7 +730,7 @@
             jax.ShapeDtypeStruct((LOADS, NY, NZ), f32),
             jax.ShapeDtypeStruct((NY, NZ), f32),
         ),
-        in_specs=[vmem] + [pl.BlockSpec(memory_space=pltpu.HBM)] * 4,
+        in_specs=[pl.BlockSpec(memory_space=pltpu.SMEM)] + [pl.BlockSpec(memory_space=pltpu.HBM)] * 4,
         out_specs=(pl.BlockSpec(memory_space=pl.ANY), vmem),
         scratch_shapes=[
             pltpu.VMEM((48, NZ), f32),
@@ -723,8 +756,8 @@
             pltpu.VMEM((18, 16, NZ), f32),
             pltpu.VMEM((18, 16, NZ), f32),
             pltpu.VMEM((2, 16, 16, NZ), f32),
-            pltpu.VMEM((3, 16, 128), f32),
-            pltpu.VMEM((25, 16, 128), f32),
+            pltpu.VMEM((3, 8, 128), f32),
+            pltpu.VMEM((25, 8, 128), f32),
             pltpu.VMEM((2, 18 * 64, 128), f32),
             pltpu.VMEM((4, 32, NZ), f32),
             pltpu.VMEM((16, NZ), f32),
@@ -738,12 +771,29 @@
             collective_id=0, has_side_effects=True, vmem_limit_bytes=64 * 2**20
         ),
     )(
-        trig,
+        angle_index,
         density.reshape(NY, NZ),
         fixed_mask.reshape(NY, NZ),
         load_mask.reshape(NY, NZ),
         load_fields.reshape(FIELDS, NY, NZ),
     )
+    anywhere = pl.BlockSpec(memory_space=pl.ANY)
+    x, filtered = pl.pallas_call(
+        hand_on,
+        out_shape=(
+            jax.ShapeDtypeStruct((LOADS, NY, NZ), f32),
+            jax.ShapeDtypeStruct((NY, NZ), f32),
+        ),
+        in_specs=[anywhere] * 2,
+        out_specs=(anywhere, anywhere),
+        scratch_shapes=[
+            pltpu.VMEM((LOADS, NY, NZ), f32),
+            pltpu.VMEM((NY, NZ), f32),
+            pltpu.SemaphoreType.DMA((LOADS + 1,)),
+            pltpu.SemaphoreType.DMA((LOADS + 1,)),
+        ],
+        compiler_params=pltpu.CompilerParams(vmem_limit_bytes=64 * 2**20),
+    )(x, filtered)
     return x.reshape(1, LOADS, 1, NY, NZ), filtered.reshape(1, NY, NZ)
 
 

time: 74.6 us -> 69.5 us (0.932)
  local copies, waits for them, and re-layouts: 3.79 us -> 0 us
  Pallas kernels: 69 us -> 67.8 us
    pallas_call x1, Pallas kernels: 69 us -> 65.7 us  [body(): pl.pallas_call(kernel, out_shape=(jax.ShapeDtypeStruct((LOADS, NY, NZ), f...]
    unnamed x4 -> x0, local copies, waits for them, and re-layouts: 2.96 us -> none
    pallas_call x0 -> x1, Pallas kernels: none -> 2.15 us  [body(): pl.pallas_call(hand_on, out_shape=(jax.ShapeDtypeStruct((LOADS, NY, NZ),...]
    broadcast_in_dim x3 -> x0, local copies, waits for them, and re-layouts: 0.83 us -> none  [body(): trig = jnp.broadcast_to(turn[:, :, None], (2, 8, 128)).reshape(16, 128)]
where the time goes in v3:
time: 69.5 us; the launch traced here: 69.1 us
  Pallas kernels  67.8 us (98%)
  between operations  1.29 us (2%)
    pallas_call x1, Pallas kernels, body(): pl.pallas_call(kernel, out_shape=(jax.ShapeDtypeStruct((LOADS, NY, NZ), f...  65.7 us
    pallas_call x1, Pallas kernels, body(): pl.pallas_call(hand_on, out_shape=(jax.ShapeDtypeStruct((LOADS, NY, NZ),...  2.15 us

profile of v3, /device:TPU:1, one launch (start us, length us, event | category | flops | bytes accessed | tf_op | source)
XLA Modules:
  0.0 69.1 jit_solution(15017262469715845734)
XLA Ops:
  1.3 65.7 %shard_map.68 = (f32[8,128,256]{2,1,0:T(8,128)}, f32[128,256]{1,0:T(8,128)}) custom-call(s32[1]{0:T(128)S(6)} %copy.8.angle_ref, f32[128,256]{1,0:T(8,128)} %bitcast.9, s32[128,256]{1,0:T(8,128)} %bitcast.10, s32[128,256]{1,0:T(8,128)} %bitcast.11, bf16[16,128,256]{2,1,0:T(8,128)(2,1)} %bitcast.8), custom_call_target="tpu_custom_call" | custom-call | tf_op jit(solution)/shard_map/pallas_call | solution.py:727
  67.0 2.1 %shard_map.69 = (f32[8,128,256]{2,1,0:T(8,128)}, f32[128,256]{1,0:T(8,128)}) custom-call(f32[8,128,256]{2,1,0:T(8,128)} %get-tuple-element.6.x_ref, f32[128,256]{1,0:T(8,128)} %get-tuple-element.7.f_ref), custom_call_target="tpu_custom_call" | custom-call | tf_op jit(solution)/shard_map/pallas_call | solution.py:781

commit v4 on v3

--- a/solution.py
+++ b/solution.py
@@ -482,20 +482,31 @@
                 )
                 for off in (1, 7)
             ]
+        if stage == 1:
+            mixed_vs += [
+                send(
+                    v_send.at[off],
+                    v_all.at[:, rows_here, :],
+                    K_MIXED + off - 1,
+                    at(0, off),
+                )
+                for off in (3,)
+            ]
+        if stage == 2:
+            mixed_vs += [
+                send(
+                    v_send.at[off],
+                    v_all.at[:, rows_here, :],
+                    K_MIXED + off - 1,
+                    at(0, off),
+                )
+                for off in (5,)
+            ]
         for n, c in enumerate(arriving):
             c.wait_recv()
             packed = packed + gram_in[first + n]
         first += len(group)
 
-    mixed_vs += [
-        send(
-            v_send.at[off],
-            v_all.at[:, rows_here, :],
-            K_MIXED + off - 1,
-            at(0, off),
-        )
-        for off in (3, 5)
-    ]
     packed = jnp.concatenate([packed, pltpu.roll(packed, 64, 1)], axis=0)
 
     narrow = lax.broadcasted_iota(jnp.int32, (8, 128), 1)
@@ -630,24 +641,6 @@
             mine = jnp.broadcast_to(jnp.sum(mine, axis=1, keepdims=True), (8, 128))
             for b in range(LOADS):
                 factors[(part * LOADS + a) * LOADS + b] = spread_row(mine, b)
-    for c in mixed_vs:
-        c.wait_recv()
-
-    @pl.loop(0, NY // 8)
-    def _(j):
-        rows = pl.ds(pl.multiple_of(j * 8, 8), 8)
-        for h in range(2):
-            cols = slice(128 * h, 128 * h + 128)
-            basis = [z_all[a, rows, cols] for a in range(LOADS)]
-            basis += [v_all[a, rows, cols] for a in range(LOADS)]
-            for b in range(LOADS):
-                total = factors[b] * basis[0]
-                for a in range(1, 2 * LOADS):
-                    total = total + factors[a * LOADS + b] * basis[a]
-                x_all[b, rows, cols] = total
-
-    keep = pltpu.make_async_copy(x_all, x_out, local_sem)
-    keep.start()
     for c in ss_in:
         c.wait_recv()
 
@@ -695,6 +688,24 @@
         )
         for off in range(1, GROUP)
     ]
+    for c in mixed_vs:
+        c.wait_recv()
+
+    @pl.loop(0, NY // 8)
+    def _(j):
+        rows = pl.ds(pl.multiple_of(j * 8, 8), 8)
+        for h in range(2):
+            cols = slice(128 * h, 128 * h + 128)
+            basis = [z_all[a, rows, cols] for a in range(LOADS)]
+            basis += [v_all[a, rows, cols] for a in range(LOADS)]
+            for b in range(LOADS):
+                total = factors[b] * basis[0]
+                for a in range(1, 2 * LOADS):
+                    total = total + factors[a * LOADS + b] * basis[a]
+                x_all[b, rows, cols] = total
+
+    keep = pltpu.make_async_copy(x_all, x_out, local_sem)
+    keep.start()
     keep.wait()
     for c in outs:
         c.wait_recv()

time: 69.5 us -> 69.1 us (level)
  the two profiles are of different devices: /device:TPU:1 before, /device:TPU:8 now
where the time goes in v4:
time: 69.1 us; the launch traced here: 68.9 us
  Pallas kernels  67.6 us (98%)
  between operations  1.29 us (2%)
    pallas_call x1, Pallas kernels, body(): pl.pallas_call(kernel, out_shape=(jax.ShapeDtypeStruct((LOADS, NY, NZ), f...  65.5 us
    pallas_call x1, Pallas kernels, body(): pl.pallas_call(hand_on, out_shape=(jax.ShapeDtypeStruct((LOADS, NY, NZ),...  2.15 us

profile of v4, /device:TPU:8, one launch (start us, length us, event | category | flops | bytes accessed | tf_op | source)
XLA Modules:
  0.0 68.9 jit_solution(3212140916310369734)
XLA Ops:
  1.3 65.5 %shard_map.68 = (f32[8,128,256]{2,1,0:T(8,128)}, f32[128,256]{1,0:T(8,128)}) custom-call(s32[1]{0:T(128)S(6)} %copy.8.angle_ref, f32[128,256]{1,0:T(8,128)} %bitcast.9, s32[128,256]{1,0:T(8,128)} %bitcast.10, s32[128,256]{1,0:T(8,128)} %bitcast.11, bf16[16,128,256]{2,1,0:T(8,128)(2,1)} %bitcast.8), custom_call_target="tpu_custom_call" | custom-call | tf_op jit(solution)/shard_map/pallas_call | solution.py:738
  66.8 2.1 %shard_map.69 = (f32[8,128,256]{2,1,0:T(8,128)}, f32[128,256]{1,0:T(8,128)}) custom-call(f32[8,128,256]{2,1,0:T(8,128)} %get-tuple-element.6.x_ref, f32[128,256]{1,0:T(8,128)} %get-tuple-element.7.f_ref), custom_call_target="tpu_custom_call" | custom-call | tf_op jit(solution)/shard_map/pallas_call | solution.py:792
